TPU v7x, 128 devices: a whole 4x4x4 slice. The times are simulated.
128 devices in a mesh: row: 16 (over y_lo, z, core), col: 8 (over x, y_hi).
Axes of the slice: x: 4, y: 4 (y_hi: 2, y_lo: 2; y = y_hi * 2 + y_lo), z: 4, core: 2. Of those that a mesh axis runs over, the one named last changes fastest.
Arguments:
- tokens: bfloat16 [2048, 8192], P('row', 'col'), may hold values from -6 to 6
- gate_weight: bfloat16 [8192, 14336], P('col', 'row'), may hold values from -0.109375 to 0.109375
- up_weight: bfloat16 [8192, 14336], P('col', 'row'), may hold values from -0.109375 to 0.109375
- down_weight: bfloat16 [14336, 8192], P('row', 'col'), may hold values from -0.09375 to 0.09375
- input_mask: int32 [64, 112], P('col', 'row'), may hold values from 0 to 1, as said below
- output_mask: int32 [112, 64], P('row', 'col'), may hold values from 0 to 1, as said below
- cotangent: bfloat16 [2048, 8192], P('row', 'col'), may hold values from -6 to 6
Outputs:
- output: bfloat16 [2048, 8192], P('row', 'col')
- grad_gate: float32 [8192, 14336], P('col', 'row')
- grad_up: float32 [8192, 14336], P('col', 'row')
- grad_down: float32 [14336, 8192], P('row', 'col')
Inputs may be any that keep to these rules, and one draw needn't show every extreme that they name: `input_mask`: entries are 0 or 1; some 30 percent are 1, a share that differs from one column of blocks to another. `output_mask`: entries are 0 or 1; some 30 percent are 1, a share that differs from one row of blocks to another.
All inputs are finite; a program needn't handle non-finite values.
Results may differ from a plain program's by a relative error of at most 0.0049.
Values may be sent and summed in bfloat16 or wider, within the bound.
A program may use at most 192 MiB of HBM per device.

v0:
```python
import jax
import jax.numpy as jnp
from jax import lax
from jax.sharding import PartitionSpec as P

BLK = 128


def expand(mask):
    return jnp.repeat(jnp.repeat(mask, BLK, axis=0), BLK, axis=1) > 0


def contract(left, right, right_axis):
    return lax.dot_general(
        left, right, (((1,), (right_axis,)), ((), ())), preferred_element_type=jnp.float32
    )


def col_share(left, right, right_axis):
    return lax.psum_scatter(
        contract(left, right, right_axis), "col", scatter_dimension=0, tiled=True
    )


def row_share(left, right, right_axis):
    return lax.psum_scatter(
        contract(left, right, right_axis), "row", scatter_dimension=0, tiled=True
    )


def activate(gate_up, width):
    gate = gate_up[:, :width]
    upper = gate_up[:, width:]
    sigma = jax.nn.sigmoid(gate)
    swish = gate * sigma
    hidden = (swish * upper).astype(jnp.bfloat16)
    return (hidden, gate, upper, sigma, swish)


def gradients(grad_hidden, gate, upper, sigma, swish):
    gate_pre = (grad_hidden * upper * sigma * (1.0 + gate * (1.0 - sigma))).astype(jnp.bfloat16)
    up_pre = (grad_hidden * swish).astype(jnp.bfloat16)
    return jnp.concatenate([gate_pre, up_pre], axis=1)


def shards(tokens, gate_weight, up_weight, down_weight, input_mask, output_mask, cotangent):
    width = gate_weight.shape[1]
    keep_in = expand(input_mask)
    keep_out = expand(output_mask)
    nothing = jnp.zeros((), jnp.bfloat16)
    both_kept = jnp.concatenate(
        [jnp.where(keep_in, gate_weight, nothing), jnp.where(keep_in, up_weight, nothing)], axis=1
    )
    down_kept = jnp.where(keep_out, down_weight, nothing)
    token_full, cotan_full = (
        lax.all_gather(tokens, "row", axis=0, tiled=True),
        lax.all_gather(cotangent, "row", axis=0, tiled=True),
    )
    gate_up = col_share(token_full, both_kept, 0)
    hidden, gate, upper, sigma, swish = activate(gate_up, width)
    hidden_full = lax.all_gather(hidden, "col", axis=0, tiled=True)
    grad_hidden = col_share(cotan_full, down_kept, 1)
    grads_local = gradients(grad_hidden, gate, upper, sigma, swish)
    grads_full = lax.all_gather(grads_local, "col", axis=0, tiled=True)
    output = row_share(hidden_full, down_kept, 0).astype(jnp.bfloat16)
    zero = jnp.zeros((), jnp.float32)
    outer = (((0,), (0,)), ((), ()))
    grad_down = jnp.where(
        keep_out,
        lax.dot_general(hidden_full, cotan_full, outer, preferred_element_type=jnp.float32),
        zero,
    )
    grad_both = lax.dot_general(token_full, grads_full, outer, preferred_element_type=jnp.float32)
    grad_gate = jnp.where(keep_in, grad_both[:, :width], zero)
    grad_up = jnp.where(keep_in, grad_both[:, width:], zero)
    return (output, grad_gate, grad_up, grad_down)


def solution(mesh):
    placed = (
        P("row", "col"),
        P("col", "row"),
        P("col", "row"),
        P("row", "col"),
        P("col", "row"),
        P("row", "col"),
        P("row", "col"),
    )
    return jax.shard_map(
        shards,
        mesh=mesh,
        in_specs=placed,
        out_specs=(P("row", "col"), P("col", "row"), P("col", "row"), P("row", "col")),
        check_vma=False,
    )
```

profile of v0, /device:TPU:0, one launch (start us, length us, event | category | flops | bytes accessed | tf_op | source)
XLA Modules:
  0.0 644.0 jit_solution(10627692270588699237)
XLA Ops:
  7.2 0.7 all-gather.9.cloned.1.call-update
  7.9 0.7 all-gather.5.cloned.1.call-update
  8.7 0.7 broadcast_compare_fusion
  9.4 40.3 %all-gather.9.cloned.1.call-done = bf16[2048,1024]{1,0:T(8,128)(2,1)} async-done(((bf16[128,1024]{1,0:T(8,128)(2,1)}), bf16[2048,1024]{1,0:T(8,128)(2,1)}) %all-gather.9.cloned.1.call-update) | async-done | bytes 4194320 | tf_op jit(solution)/shard_map/all_gather | solution.py:57
  49.7 2.8 broadcast_in_dim.34
  52.5 9.7 %convolution_bitcast_fusion.2 = f32[2048,896]{0,1:T(8,128)} fusion(bf16[2048,1024]{1,0:T(8,128)(2,1)} %all-gather.9.cloned.1.call-done, bf16[896,1024]{1,0:T(8,128)(2,1)} %param.10, pred[112,8,8,128]{3,2,1,0:T(8,128)(4,1)S(1)} %bitcast.32), kind=kOutput, calls=%fused_computation.6 | convolution fusion | flops 3759013888 | bytes 14286848 | tf_op jit(solution)/shard_map/dot_general | solution.py:14
  62.2 0.0 reduce-scatter.4.cloned.1.call-start
  62.2 0.6 copy-done
  62.9 0.1 copy.11
  63.0 0.1 broadcast_bitcast_fusion
  63.0 2.9 copy.12
  66.0 3.8 copy.13
  69.8 3.6 bitcast_select_fusion.3
  73.4 15.4 %all-gather.5.cloned.1.call-done = bf16[2048,1024]{1,0:T(8,128)(2,1)} async-done(((bf16[128,1024]{1,0:T(8,128)(2,1)}), bf16[2048,1024]{1,0:T(8,128)(2,1)}) %all-gather.5.cloned.1.call-update) | async-done | bytes 4194320 | tf_op jit(solution)/shard_map/all_gather | solution.py:56
  88.8 13.8 %convolution_bitcast_fusion = f32[2048,1792]{0,1:T(8,128)} fusion(bf16[2048,1024]{1,0:T(8,128)(2,1)} %all-gather.5.cloned.1.call-done, bf16[1024,896]{0,1:T(8,128)(2,1)} %get-tuple-element.14, bf16[1024,896]{0,1:T(8,128)(2,1)} %get-tuple-element.13), kind=kOutput, calls=%fused_computation.4 | convolution fusion | flops 7523532800 | bytes 22544384 | tf_op jit(solution)/shard_map/dot_general | solution.py:14
  102.7 0.0 all-gather.7.cloned.1.call-start
  102.7 98.4 %reduce-scatter.8.cloned.1.call-done = f32[256,896]{0,1:T(8,128)} async-done(((f32[2048,896]{0,1:T(8,128)}), f32[256,896]{0,1:T(8,128)}) %reduce-scatter.8.cloned.1.call-update) | async-done | bytes 917520 | tf_op jit(solution)/shard_map/reduce_scatter | solution.py:20
  201.1 172.7 %reduce-scatter.4.cloned.1.call-done = f32[256,1792]{0,1:T(8,128)} async-done(((f32[2048,1792]{0,1:T(8,128)}), f32[256,1792]{0,1:T(8,128)}) %reduce-scatter.4.cloned.1.call-update) | async-done | bytes 1835024 | tf_op jit(solution)/shard_map/reduce_scatter | solution.py:20
  373.9 3.0 multiply_convert_fusion.1
  376.9 0.0 all-gather.11.cloned.1.call-start
  376.9 1.0 pad_maximum_fusion
  377.9 0.2 reduce-scatter.6.cloned.1.call-start
  378.2 69.6 %all-gather.7.cloned.1.call-done = bf16[2048,896]{0,1:T(8,128)(2,1)} async-done(((bf16[256,896]{0,1:T(8,128)(2,1)}), bf16[2048,896]{0,1:T(8,128)(2,1)}) %all-gather.7.cloned.1.call-update) | async-done | bytes 3670032 | tf_op jit(solution)/shard_map/all_gather | solution.py:61
  447.7 10.5 %fusion.3 = f32[2048,1024]{1,0:T(8,128)} fusion(bf16[2048,896]{0,1:T(8,128)(2,1)} %all-gather.7.cloned.1.call-done, bf16[896,1024]{1,0:T(8,128)(2,1)} %param.10, pred[112,8,8,128]{3,2,1,0:T(8,128)(4,1)S(1)} %bitcast.33), kind=kOutput, calls=%fused_computation.12 | convolution fusion | flops 3759013888 | bytes 14811136 | tf_op jit(solution)/shard_map/dot_general | solution.py:14
  458.2 9.7 %bitcast_select_fusion.4 = f32[896,1024]{1,0:T(8,128)} fusion(pred[112,8,8,128]{3,2,1,0:T(8,128)(4,1)S(1)} %bitcast.34, bf16[2048,896]{0,1:T(8,128)(2,1)} %all-gather.7.cloned.1.call-done, bf16[2048,1024]{1,0:T(8,128)(2,1)} %all-gather.9.cloned.1.call-done), kind=kOutput, calls=%fused_computation.10 | convolution fusion | flops 3759013888 | bytes 12451840 | tf_op jit(solution)/shard_map/dot_general | solution.py:70
  467.9 91.2 %all-gather.11.cloned.1.call-done = bf16[2048,1792]{0,1:T(8,128)(2,1)} async-done(((bf16[256,1792]{0,1:T(8,128)(2,1)}), bf16[2048,1792]{0,1:T(8,128)(2,1)}) %all-gather.11.cloned.1.call-update) | async-done | bytes 7340048 | tf_op jit(solution)/shard_map/all_gather | solution.py:64
  559.1 11.2 %convolution_bitcast_fusion.1 = f32[1024,1792]{0,1:T(8,128)S(1)} fusion(bf16[2048,1792]{0,1:T(8,128)(2,1)} %all-gather.11.cloned.1.call-done, bf16[2048,1024]{1,0:T(8,128)(2,1)} %all-gather.5.cloned.1.call-done), kind=kOutput, calls=%fused_computation.5 | convolution fusion | flops 7516192768 | bytes 18874368 | tf_op jit(solution)/shard_map/dot_general | solution.py:73
  570.3 4.8 bitcast_select_fusion
  575.1 5.1 copy.14
  580.1 5.0 copy.15
  585.2 50.2 %reduce-scatter.6.cloned.1.call-done = f32[128,1024]{1,0:T(8,128)} async-done(((f32[2048,1024]{1,0:T(8,128)}), f32[128,1024]{1,0:T(8,128)}) %reduce-scatter.6.cloned.1.call-update) | async-done | bytes 524304 | tf_op jit(solution)/shard_map/reduce_scatter | solution.py:26
  635.4 1.8 convert_element_type.13
  (12 shorter events, 0.2 us)
Async XLA Ops:
  7.2 42.5 %all-gather.9.cloned.1.call-start = ((), (), s32[]{:S(2)}) async-start(), calls=%async_computation.7 | async-start | bytes 4456448 | tf_op jit(solution)/shard_map/all_gather | solution.py:57
  7.9 80.9 %all-gather.5.cloned.1.call-start = ((), (), s32[]{:S(2)}) async-start(), calls=%async_computation.3 | async-start | bytes 4456448 | tf_op jit(solution)/shard_map/all_gather | solution.py:56
  8.6 192.5 %reduce-scatter.8.cloned.1.call-start = ((), (), s32[]{:S(2)}) async-start(), calls=%async_computation.8 | async-start | bytes 8257536 | tf_op jit(solution)/shard_map/reduce_scatter | solution.py:20
  62.2 0.7 copy-start
  62.2 311.7 %reduce-scatter.4.cloned.1.call-start = ((), (), s32[]{:S(2)}) async-start(), calls=%async_computation.4 | async-start | bytes 16515072 | tf_op jit(solution)/shard_map/reduce_scatter | solution.py:20
  102.7 345.1 %all-gather.7.cloned.1.call-start = ((), (), s32[]{:S(2)}) async-start(), calls=%async_computation.5 | async-start | bytes 4128768 | tf_op jit(solution)/shard_map/all_gather | solution.py:61
  376.9 182.2 %all-gather.11.cloned.1.call-start = ((), (), s32[]{:S(2)}) async-start(), calls=%async_computation.9 | async-start | bytes 8257536 | tf_op jit(solution)/shard_map/all_gather | solution.py:64
  377.9 257.5 %reduce-scatter.6.cloned.1.call-start = ((), (), s32[]{:S(2)}) async-start(), calls=%async_computation.6 | async-start | bytes 8912896 | tf_op jit(solution)/shard_map/reduce_scatter | solution.py:26
Sparse Core Ops, SparseCore 0:
  9.7 39.8 all-gather.8
  51.4 37.4 all-gather.4
  92.7 108.3 reduce-scatter.7
  205.4 168.4 reduce-scatter.3
  377.0 70.6 all-gather.6
  450.3 108.7 all-gather.10
  561.5 73.8 reduce-scatter.5
where the time goes:
time: 645 us; the launch traced here: 644 us
  waiting for transfers between devices  539 us (84%)
  matrix products  54.9 us (9%)
  local copies, waits for them, and re-layouts  20.4 us (3%)
  other arithmetic  14.8 us (2%)
  between operations  14.2 us (2%)
    reduce_scatter x2, waiting for transfers between devices, col_share(): lax.psum_scatter(contract(left, right, right_axis), 'col', scatter_dimens...  271 us
    all_gather x1, waiting for transfers between devices, shards(): grads_full = lax.all_gather(grads_local, 'col', axis=0, tiled=True)  91.2 us
    all_gather x1, waiting for transfers between devices, shards(): hidden_full = lax.all_gather(hidden, 'col', axis=0, tiled=True)  69.6 us
    reduce_scatter x1, waiting for transfers between devices, row_share(): lax.psum_scatter(contract(left, right, right_axis), 'row', scatter_dimens...  50.2 us
    all_gather x1, waiting for transfers between devices, shards(): lax.all_gather(cotangent, 'row', axis=0, tiled=True)  40.3 us
    dot_general x3, matrix products, contract(): lax.dot_general(left, right, (((1,), (right_axis,)), ((), ())), preferred...  33.9 us
    unnamed x8, local copies, waits for them, and re-layouts  17.5 us
    all_gather x1, waiting for transfers between devices, shards(): lax.all_gather(tokens, 'row', axis=0, tiled=True)  15.4 us
  transfers between devices with their start and end apart: 7, of which 7 were waited for; matrix products, arithmetic and copies ran while one was open for 13% of the time, Pallas kernels for 0%

commit v1 on v0

v1 whole, which is shorter than its diff:
```python
import jax
import jax.numpy as jnp
from jax import lax
from jax.experimental import pallas as pl
from jax.experimental.pallas import tpu as pltpu
from jax.sharding import PartitionSpec as P

BLK = 128
BF = jnp.bfloat16
F32 = jnp.float32
MESH = pl.DeviceIdType.MESH
VMEM_LIMIT = 62 * 2**20
SLOTS = 96


def aligned(start, size, to=128):
    return pl.ds(pl.multiple_of(start, to), size)


def forward_kernel(
    tok, cot, gate_w, up_w, down_w, keep_in, keep_out,
    out, tok_hbm, cot_hbm, hid_hbm, grd_hbm,
    w_in, w_down, tok_all, cot_all,
    u_s2, u_sp, u_sm, u_ia, u_ib, u_rp, u_rm, u_ys, u_yr, u_own,
    h_s2, h_sp, h_sm, h_ia, h_ib, h_rp, h_rm, h_ys, h_yr, h_own,
    hid_own, grd_own, hid_all,
    c_s, c_r, z_s2, z_i, z_sp, z_sm, z_rp, z_rm, o_ys, o_yr, o_own,
    send_sem, recv_sem, local_sem,
):
    row = lax.axis_index("row")
    col = lax.axis_index("col")
    x, h = col // 2, col % 2
    yl, z, c = row // 8, (row // 2) % 4, row % 2

    def device(x_, h_, yl_, z_, c_):
        return (yl_ * 8 + z_ * 2 + c_, x_ * 2 + h_)

    xp = device((x + 1) % 4, h, yl, z, c)
    xm = device((x + 3) % 4, h, yl, z, c)
    yh = device(x, 1 - h, yl, z, c)
    yn = device(x, h, 1 - yl, z, c)
    zp = device(x, h, yl, (z + 1) % 4, c)
    zm = device(x, h, yl, (z + 3) % 4, c)
    co = device(x, h, yl, z, 1 - c)
    peers = (xp, xm, yh, yn, zp, zm, co)

    slot = [0]
    sent = []

    def send(src, dst, peer):
        i = slot[0]
        slot[0] += 1
        copy = pltpu.make_async_remote_copy(
            src_ref=src, dst_ref=dst, send_sem=send_sem.at[i], recv_sem=recv_sem.at[i],
            device_id=peer, device_id_type=MESH,
        )
        copy.start()
        sent.append(copy)
        return copy

    locals_ = [0]

    def local(src, dst):
        copy = pltpu.make_async_copy(src, dst, local_sem.at[locals_[0]])
        locals_[0] += 1
        copy.start()
        return copy

    loads = [
        local(gate_w, w_in.at[:, 0:896]),
        local(up_w, w_in.at[:, 896:1792]),
        local(down_w, w_down),
    ]

    barrier = pltpu.get_barrier_semaphore()
    for peer in peers:
        pl.semaphore_signal(barrier, inc=1, device_id=peer, device_id_type=MESH)
    pl.semaphore_wait(barrier, len(peers))

    def block(yl_, z_, c_):
        return yl_ * 8 + z_ * 2 + c_

    def rows(b, part=0, size=128):
        return aligned(b * 128 + part * 64, size, 64)

    def gather_row(own, whole):
        me = block(yl, z, c)
        spot = whole.at[rows(me)]
        to_y = send(own, spot, yn)
        own_p, own_m = send(own, spot, zp), send(own, spot, zm)
        cores = [send(own, spot, co)]
        whole[rows(me), :] = own[...]
        yield
        to_y.wait_recv()
        spot = whole.at[rows(block(1 - yl, z, c))]
        mate_p, mate_m = send(spot, spot, zp), send(spot, spot, zm)
        cores.append(send(spot, spot, co))
        halves = []
        for y_, from_m, from_p in ((yl, own_p, own_m), (1 - yl, mate_p, mate_m)):
            from_m.wait_recv()
            b = block(y_, (z + 3) % 4, c)
            spot = whole.at[rows(b, 0, 64)]
            first = send(spot, spot, zp)
            spot = whole.at[rows(b)]
            cores.append(send(spot, spot, co))
            from_p.wait_recv()
            b = block(y_, (z + 1) % 4, c)
            spot = whole.at[rows(b, 1, 64)]
            second = send(spot, spot, zm)
            spot = whole.at[rows(b)]
            cores.append(send(spot, spot, co))
            halves.append((y_, first, second))
        yield
        for y_, first, second in halves:
            first.wait_recv()
            second.wait_recv()
            spot = whole.at[rows(block(y_, (z + 2) % 4, c))]
            cores.append(send(spot, spot, co))
        for copy in cores:
            copy.wait_recv()
        yield

    tok_steps = gather_row(tok, tok_all)
    cot_steps = gather_row(cot, cot_all)
    next(tok_steps)

    for copy in loads:
        copy.wait()
    for i in range(8):
        at = slice(i * 128, i * 128 + 128)
        for j in range(2):
            cols = slice(j * 896, j * 896 + 896)
            w_in[at, cols] = jnp.where(
                keep_in[i : i + 1, :] > 0, w_in[at, cols].astype(F32), 0.0
            ).astype(BF)
    for i in range(7):
        at = slice(i * 128, i * 128 + 128)
        w_down[at, :] = jnp.where(
            keep_out[i : i + 1, :] > 0, w_down[at, :].astype(F32), 0.0
        ).astype(BF)

    next(tok_steps)
    next(cot_steps)
    next(tok_steps)
    stores = [local(tok_all, tok_hbm)]

    def gate_up(chunk, half, emit):
        lhs = aligned(chunk * 512 + half * 256, 256, 256)

        @pl.loop(0, 7)
        def _(t):
            cols = aligned(t * 256, 256, 256)
            emit(jnp.dot(tok_all[lhs, :], w_in[:, cols], preferred_element_type=F32), cols)

    def grad_hidden(chunk, half, emit):
        lhs = aligned(chunk * 512 + half * 256, 256, 256)

        def tile(start, size):
            emit(
                lax.dot_general(
                    cot_all[lhs, :], w_down[aligned(start, size), :],
                    (((1,), (1,)), ((), ())), preferred_element_type=F32,
                ),
                aligned(start, size),
            )

        @pl.loop(0, 3)
        def _(t):
            tile(t * 256, 256)

        tile(768, 128)

    def put(buf, half):
        def emit(v, cols):
            buf[half * 256 : half * 256 + 256, cols] = v.astype(BF)
        return emit

    def put_sum(buf, half, inc):
        def emit(v, cols):
            buf[half * 256 : half * 256 + 256, cols] = (v + inc[:, cols].astype(F32)).astype(BF)
        return emit

    def reduce_col(product, s2, sp, sm, ia, ib, rp, rm, ys, yr, own):
        far, after, before = (x + 2) % 4, (x + 1) % 4, (x + 3) % 4
        lo, hi = slice(0, 256), slice(256, 512)
        product(far, 0, put(s2, 0))
        mid_a = send(s2.at[lo], ia, xp)
        product(far, 1, put(s2, 1))
        mid_b = send(s2.at[hi], ib, xm)
        product(after, 1, put(sp, 1))
        fin = [send(sp.at[hi], rp.at[hi], xp)]
        product(before, 0, put(sm, 0))
        fin.append(send(sm.at[lo], rm.at[lo], xm))
        yield
        mid_a.wait_recv()
        product(after, 0, put_sum(sp, 0, ia))
        fin.append(send(sp.at[lo], rp.at[lo], xp))
        mid_b.wait_recv()
        product(before, 1, put_sum(sm, 1, ib))
        fin.append(send(sm.at[hi], rm.at[hi], xm))
        yield
        for copy in fin:
            copy.wait_recv()

        def emit_total(half, target):
            at = aligned(half * 256, 256, 256)

            def emit(v, cols):
                total = v + rp[at, cols].astype(F32) + rm[at, cols].astype(F32)
                target[:, cols] = total.astype(target.dtype)
            return emit

        product(x, 1 - h, emit_total(1 - h, ys))
        over = send(ys, yr, yh)
        product(x, h, emit_total(h, own))
        yield
        over.wait_recv()
        yield

    def gather_col(own, whole):
        def spot_of(x_, h_, part=0, size=256):
            return whole.at[aligned(x_ * 512 + h_ * 256 + part * 128, size)]

        spot = spot_of(x, h)
        to_y = send(own, spot, yh)
        own_p, own_m = send(own, spot, xp), send(own, spot, xm)
        mine = local(own, spot)
        yield
        to_y.wait_recv()
        spot = spot_of(x, 1 - h)
        mate_p, mate_m = send(spot, spot, xp), send(spot, spot, xm)
        yield
        halves = []
        for h_, from_m, from_p in ((h, own_p, own_m), (1 - h, mate_p, mate_m)):
            from_m.wait_recv()
            spot = spot_of((x + 3) % 4, h_, 0, 128)
            halves.append(send(spot, spot, xp))
            from_p.wait_recv()
            spot = spot_of((x + 1) % 4, h_, 1, 128)
            halves.append(send(spot, spot, xm))
            yield
        for copy in halves:
            copy.wait_recv()
        mine.wait()
        yield

    up_steps = reduce_col(gate_up, u_s2, u_sp, u_sm, u_ia, u_ib, u_rp, u_rm, u_ys, u_yr, u_own)
    gh_steps = reduce_col(grad_hidden, h_s2, h_sp, h_sm, h_ia, h_ib, h_rp, h_rm, h_ys, h_yr, h_own)
    next(up_steps)
    next(cot_steps)
    next(cot_steps)
    stores.append(local(cot_all, cot_hbm))
    next(up_steps)
    next(gh_steps)
    next(up_steps)
    next(gh_steps)
    next(up_steps)

    @pl.loop(0, 16)
    def _(t):
        at = aligned(t * 16, 16, 16)
        gate = u_own[at, 0:896] + u_yr[at, 0:896].astype(F32)
        upper = u_own[at, 896:1792] + u_yr[at, 896:1792].astype(F32)
        sigma = 1.0 / (1.0 + jnp.exp(-gate))
        swish = gate * sigma
        hid_own[at, :] = (swish * upper).astype(BF)
        u_own[at, 0:896] = upper * sigma * (1.0 + gate * (1.0 - sigma))
        u_own[at, 896:1792] = swish

    hid_steps = gather_col(hid_own, hid_all)
    next(hid_steps)
    next(gh_steps)
    next(hid_steps)
    next(hid_steps)
    next(gh_steps)

    @pl.loop(0, 16)
    def _(t):
        at = aligned(t * 16, 16, 16)
        grad = h_own[at, :] + h_yr[at, :].astype(F32)
        grd_own[at, 0:896] = (grad * u_own[at, 0:896]).astype(BF)
        grd_own[at, 896:1792] = (grad * u_own[at, 896:1792]).astype(BF)

    grd_steps = gather_col(grd_own, grd_hbm)
    next(grd_steps)
    next(hid_steps)
    next(hid_steps)
    stores.append(local(hid_all, hid_hbm))

    def output_of(b):
        return jnp.dot(hid_all[rows(b), :], w_down[...], preferred_element_type=F32)

    def kept(yl_, z_):
        def piece(cols):
            part = jnp.dot(
                hid_all[rows(block(yl_, z_, c)), :], w_down[:, cols], preferred_element_type=F32
            )
            return part + c_r[yl_ * 4 + z_, :, cols]
        return piece

    def over_cols(body):
        @pl.loop(0, 4)
        def _(t):
            body(aligned(t * 256, 256, 256))

    for y_ in range(2):
        @pl.loop(0, 4)
        def _(z_):
            def body(cols):
                c_s[y_ * 4 + z_, :, cols] = jnp.dot(
                    hid_all[rows(block(y_, z_, 1 - c)), :], w_down[:, cols],
                    preferred_element_type=F32,
                )
            over_cols(body)

        if y_ == 0:
            core_0 = send(c_s.at[0:4], c_r.at[0:4], co)
        else:
            core_1 = send(c_s.at[4:8], c_r.at[4:8], co)

    next(grd_steps)
    core_0.wait_recv()
    core_1.wait_recv()
    far, after, before = (z + 2) % 4, (z + 1) % 4, (z + 3) % 4

    def ring_piece(y_, z_, target, inc=None):
        piece = kept(y_, z_)

        def body(cols):
            v = piece(cols)
            if inc is not None:
                v = v + inc[:, cols]
            target[:, cols] = v
        over_cols(body)

    ring_piece(0, far, z_s2.at[0])
    z_mid_a = send(z_s2.at[0], z_i.at[0], zp)
    ring_piece(1, far, z_s2.at[1])
    z_mid_b = send(z_s2.at[1], z_i.at[1], zm)
    ring_piece(1, after, z_sp.at[1])
    z_fin = [send(z_sp.at[1], z_rp.at[1], zp)]
    ring_piece(0, before, z_sm.at[0])
    z_fin.append(send(z_sm.at[0], z_rm.at[0], zm))
    next(grd_steps)
    z_mid_a.wait_recv()
    ring_piece(0, after, z_sp.at[0], z_i.at[0])
    z_fin.append(send(z_sp.at[0], z_rp.at[0], zp))
    z_mid_b.wait_recv()
    ring_piece(1, before, z_sm.at[1], z_i.at[1])
    z_fin.append(send(z_sm.at[1], z_rm.at[1], zm))
    next(grd_steps)
    for copy in z_fin:
        copy.wait_recv()

    def row_total(y_, target):
        piece = kept(y_, z)

        def body(cols):
            target[:, cols] = piece(cols) + z_rp[y_, :, cols] + z_rm[y_, :, cols]
        over_cols(body)

    row_total(1 - yl, o_ys)
    o_over = send(o_ys, o_yr, yn)
    row_total(yl, o_own)
    o_over.wait_recv()
    out[...] = (o_own[...] + o_yr[...]).astype(BF)
    next(grd_steps)
    for copy in stores:
        copy.wait()
    for copy in sent:
        copy.wait_send()


def forward(tokens, cotangent, gate_weight, up_weight, down_weight, keep_in, keep_out):
    hbm = pl.BlockSpec(memory_space=pl.ANY)
    vmem = pl.BlockSpec(memory_space=pltpu.VMEM)

    def bf(*shape):
        return pltpu.VMEM(shape, BF)

    def f32(*shape):
        return pltpu.VMEM(shape, F32)

    def ring(w):
        return [
            bf(512, w), bf(512, w), bf(512, w), bf(256, w), bf(256, w), bf(512, w), bf(512, w),
            bf(256, w), bf(256, w), f32(256, w),
        ]

    sds = jax.ShapeDtypeStruct
    return pl.pallas_call(
        forward_kernel,
        out_shape=(
            sds((128, 1024), BF), sds((2048, 1024), BF), sds((2048, 1024), BF),
            sds((2048, 896), BF), sds((2048, 1792), BF),
        ),
        in_specs=[vmem, vmem, hbm, hbm, hbm, vmem, vmem],
        out_specs=[vmem, hbm, hbm, hbm, hbm],
        scratch_shapes=[bf(1024, 1792), bf(896, 1024), bf(2048, 1024), bf(2048, 1024)]
        + ring(1792)
        + ring(896)
        + [bf(256, 896), bf(256, 1792), bf(2048, 896)]
        + [f32(8, 128, 1024), f32(8, 128, 1024)]
        + [f32(2, 128, 1024)] * 6
        + [f32(128, 1024)] * 3
        + [
            pltpu.SemaphoreType.DMA((SLOTS,)), pltpu.SemaphoreType.DMA((SLOTS,)),
            pltpu.SemaphoreType.DMA((8,)),
        ],
        compiler_params=pltpu.CompilerParams(
            collective_id=0, has_side_effects=True, vmem_limit_bytes=VMEM_LIMIT
        ),
    )(tokens, cotangent, gate_weight, up_weight, down_weight, keep_in, keep_out)


def expand(mask):
    return jnp.repeat(jnp.repeat(mask, BLK, axis=0), BLK, axis=1) > 0


def shards(tokens, gate_weight, up_weight, down_weight, input_mask, output_mask, cotangent):
    width = gate_weight.shape[1]
    lanes_in = jnp.repeat(input_mask.astype(F32), BLK, axis=1)
    lanes_out = jnp.repeat(output_mask.astype(F32), BLK, axis=1)
    output, tok_all, cot_all, hid_all, grd_all = forward(
        tokens, cotangent, gate_weight, up_weight, down_weight, lanes_in, lanes_out
    )
    keep_in, keep_out = expand(input_mask), expand(output_mask)
    outer = (((0,), (0,)), ((), ()))

    def grad(left, right, keep):
        full = lax.dot_general(left, right, outer, preferred_element_type=F32)
        return jnp.where(keep, full, jnp.zeros((), F32))

    grad_down = grad(hid_all, cot_all, keep_out)
    grad_gate = grad(tok_all, grd_all[:, :width], keep_in)
    grad_up = grad(tok_all, grd_all[:, width:], keep_in)
    return (output, grad_gate, grad_up, grad_down)


def solution(mesh):
    placed = (
        P("row", "col"), P("col", "row"), P("col", "row"), P("row", "col"),
        P("col", "row"), P("row", "col"), P("row", "col"),
    )
    return jax.shard_map(
        shards, mesh=mesh, in_specs=placed,
        out_specs=(P("row", "col"), P("col", "row"), P("col", "row"), P("row", "col")),
        check_vma=False,
    )
```

time: 645 us -> 272 us (0.42)
  waiting for transfers between devices: 539 us -> 0 us
  Pallas kernels: 0 us -> 240 us
  matrix products: 54.9 us -> 22.1 us
  local copies, waits for them, and re-layouts: 20.4 us -> 6.46 us
  between operations: 14.2 us -> 0.69 us
  other arithmetic: 14.8 us -> 2.76 us
    reduce_scatter x3 -> x0, waiting for transfers between devices: 321 us -> none  [the longest x2 271 us: col_share(): lax.psum_scatter(contract(left, right, right_axis), 'col', scatter_dimens...]
    pallas_call x0 -> x1, Pallas kernels: none -> 240 us  [forward(): pl.pallas_call(forward_kernel, out_shape=(sds((128, 1024), BF), sds((2048...]
    all_gather x4 -> x0, waiting for transfers between devices: 216 us -> none  [the longest x1 91.2 us: shards(): grads_full = lax.all_gather(grads_local, 'col', axis=0, tiled=True)]
    dot_general x5 -> x3, matrix products: 54.9 us -> 22.1 us  [grad(): full = lax.dot_general(left, right, outer, preferred_element_type=F32)]
    unnamed x8 -> x11, local copies, waits for them, and re-layouts: 17.5 us -> 1.5 us
    select_n x2 -> x0, other arithmetic: 8.39 us -> none  [the longest x1 4.75 us: shards(): grad_up = jnp.where(keep_in, grad_both[:, width:], zero)]
  transfers between devices with their start and end apart: 7 -> 0, of which waited for: 7 -> 0; matrix products, arithmetic and copies ran while one was open for 13% -> 0% of each run, Pallas kernels for 0% -> 0%
where the time goes in v1:
time: 272 us
  Pallas kernels  240 us (88%)
  matrix products  22.1 us (8%)
  local copies, waits for them, and re-layouts  6.46 us (2%)
  other arithmetic  2.76 us (1%)
    pallas_call x1, Pallas kernels, forward(): pl.pallas_call(forward_kernel, out_shape=(sds((128, 1024), BF), sds((2048...  240 us
    dot_general x3, matrix products, grad(): full = lax.dot_general(left, right, outer, preferred_element_type=F32)  22.1 us

profile of v1, /device:TPU:0, one launch (start us, length us, event | category | flops | bytes accessed | tf_op | source)
XLA Modules:
  0.0 271.6 jit_solution(7045093076159269988)
XLA Ops:
  0.6 0.7 broadcast_compare_fusion.1
  1.3 0.1 copy.13
  1.4 0.7 broadcast_compare_fusion
  2.1 0.7 convert_element_type.6
  2.8 0.1 copy.12
  2.9 0.7 convert_element_type.7
  3.6 0.1 broadcast_bitcast_fusion.2
  3.7 0.1 broadcast_bitcast_fusion
  3.7 0.6 copy.22
  4.4 0.7 broadcast_bitcast_fusion.1.keep_in
  5.1 2.8 %broadcast_in_dim.33 = pred[896,8,128]{2,1,0:T(8,128)(4,1)S(1)} broadcast(pred[896,8]{1,0:T(8,128)(4,1)S(1)} %bitcast.25), dimensions={0,1} | broadcast | bytes 924672 | tf_op jit(solution)/shard_map/broadcast_in_dim | solution.py:417
  7.9 0.2 broadcast_in_dim.30
  8.1 1.0 copy.14
  9.2 239.5 %shard_map.102 = (bf16[128,1024]{1,0:T(8,128)(2,1)}, bf16[2048,1024]{1,0:T(8,128)(2,1)}, bf16[2048,1024]{1,0:T(8,128)(2,1)}, bf16[2048,896]{1,0:T(8,128)(2,1)}, bf16[2048,1792]{1,0:T(8,128)(2,1)}) custom-call(bf16[128,1024]{1,0:T(8,128)(2,1)} %tok.1, bf16[128,1024]{1,0:T(8,128)(2,1)} %cot.1, bf16[1024,896]{1,0:T(8,128)(2,1)} %gate_w.1, ...), custom_call_target="tpu_custom_call" | custom-call | tf_op jit(solution)/shard_map/pallas_call | solution.py:391
  248.7 0.0 copy-start.1
  248.7 0.0 copy-start.2
  248.7 9.4 %bitcast_select_fusion = f32[896,1024]{1,0:T(8,128)} fusion(pred[112,8,8,128]{3,2,1,0:T(8,128)(4,1)S(1)} %bitcast.24, bf16[2048,896]{1,0:T(8,128)(2,1)} %get-tuple-element.12, bf16[2048,1024]{1,0:T(8,128)(2,1)} %get-tuple-element.13), kind=kOutput, calls=%fused_computation.4 | convolution fusion | flops 3759013888 | bytes 12451840 | tf_op jit(solution)/shard_map/dot_general | solution.py:431
  258.1 0.0 copy-done.1
  258.1 0.0 copy-done.2
  258.1 6.4 %broadcast_select_fusion = f32[1024,896]{1,0:T(8,128)} fusion(pred[1024,896]{1,0:T(32,128)(4,1)S(1)} %copy.14, bf16[2048,1024]{1,0:T(8,128)(2,1)S(1)} %copy-done.2, bf16[2048,1792]{1,0:T(8,128)(2,1)S(1)} %copy-done.1), kind=kOutput, calls=%fused_computation.5 | convolution fusion | flops 3759013888 | bytes 12451840 | tf_op jit(solution)/shard_map/dot_general | solution.py:431
  264.5 0.0 copy-start
  264.5 6.4 %broadcast_select_fusion.1 = f32[1024,896]{1,0:T(8,128)} fusion(pred[1024,896]{1,0:T(32,128)(4,1)S(1)} %copy.14, bf16[2048,1024]{1,0:T(8,128)(2,1)S(1)} %copy-done.2, bf16[2048,1792]{1,0:T(8,128)(2,1)S(1)} %copy-done.1), kind=kOutput, calls=%fused_computation.6 | convolution fusion | flops 3759013888 | bytes 12451840 | tf_op jit(solution)/shard_map/dot_general | solution.py:431
  270.9 0.0 copy-done
  270.9 0.7 copy.27
  (2 shorter events, 0.0 us)
Async XLA Ops:
  248.7 9.4 %copy-start.1 = (bf16[2048,1792]{1,0:T(8,128)(2,1)S(1)}, bf16[2048,1792]{1,0:T(8,128)(2,1)}, u32[]{:S(2)}) copy-start(bf16[2048,1792]{1,0:T(8,128)(2,1)} %get-tuple-element.11) | copy-start | bytes 22020100
  248.7 9.4 %copy-start.2 = (bf16[2048,1024]{1,0:T(8,128)(2,1)S(1)}, bf16[2048,1024]{1,0:T(8,128)(2,1)}, u32[]{:S(2)}) copy-start(bf16[2048,1024]{1,0:T(8,128)(2,1)} %get-tuple-element.10) | copy-start | bytes 12582916
  264.5 6.4 %copy-start = (bf16[128,1024]{1,0:T(8,128)(2,1)S(1)}, bf16[128,1024]{1,0:T(8,128)(2,1)}, u32[]{:S(2)}) copy-start(bf16[128,1024]{1,0:T(8,128)(2,1)} %get-tuple-element.18) | copy-start | bytes 786436

commit v2 on v1

v2 whole, which is shorter than its diff:
```python
import jax
import jax.numpy as jnp
from jax import lax
from jax.experimental import pallas as pl
from jax.experimental.pallas import tpu as pltpu
from jax.sharding import PartitionSpec as P

BLK = 128
BF = jnp.bfloat16
F32 = jnp.float32
MESH = pl.DeviceIdType.MESH
VMEM_LIMIT = 62 * 2**20
SLOTS = 112


def aligned(start, size, to=128):
    return pl.ds(pl.multiple_of(start, to), size)


def forward_kernel(
    tok, cot, gate_w, up_w, down_w, keep_in, keep_out,
    out, tok_hbm, cot_hbm, hid_hbm, gp_hbm, up_hbm,
    w_gate, w_up, w_down, tok_all, cot_all,
    g_s2, g_sp, g_sm, g_ia, g_ib, g_rp, g_rm, g_ys, g_yr, g_own,
    h_s2, h_sp, h_sm, h_ia, h_ib, h_rp, h_rm, h_ys, h_yr, h_own,
    u_ys, u_yr, u_s2, u_sp, u_sm, u_ia, u_ib, u_rp, u_rm, u_own,
    hid_own, gp_own, up_own, hid_all,
    c_s, c_r, z_s2, z_i, z_sp, z_sm, z_rp, z_rm, o_ys, o_yr, o_own,
    send_sem, recv_sem, local_sem,
):
    row = lax.axis_index("row")
    col = lax.axis_index("col")
    x, h = col // 2, col % 2
    yl, z, c = row // 8, (row // 2) % 4, row % 2

    def device(x_, h_, yl_, z_, c_):
        return (yl_ * 8 + z_ * 2 + c_, x_ * 2 + h_)

    xp = device((x + 1) % 4, h, yl, z, c)
    xm = device((x + 3) % 4, h, yl, z, c)
    yh = device(x, 1 - h, yl, z, c)
    yn = device(x, h, 1 - yl, z, c)
    zp = device(x, h, yl, (z + 1) % 4, c)
    zm = device(x, h, yl, (z + 3) % 4, c)
    co = device(x, h, yl, z, 1 - c)
    peers = (xp, xm, yh, yn, zp, zm, co)

    slot = [0]
    sent = []

    def send(src, dst, peer):
        i = slot[0]
        slot[0] += 1
        copy = pltpu.make_async_remote_copy(
            src_ref=src, dst_ref=dst, send_sem=send_sem.at[i], recv_sem=recv_sem.at[i],
            device_id=peer, device_id_type=MESH,
        )
        copy.start()
        sent.append(copy)
        return copy

    locals_ = [0]

    def local(src, dst):
        copy = pltpu.make_async_copy(src, dst, local_sem.at[locals_[0]])
        locals_[0] += 1
        copy.start()
        return copy

    loads = [local(gate_w, w_gate), local(up_w, w_up), local(down_w, w_down)]

    barrier = pltpu.get_barrier_semaphore()
    for peer in peers:
        pl.semaphore_signal(barrier, inc=1, device_id=peer, device_id_type=MESH)
    pl.semaphore_wait(barrier, len(peers))

    def block(yl_, z_, c_):
        return yl_ * 8 + z_ * 2 + c_

    def rows(b, part=0, size=128):
        return aligned(b * 128 + part * 64, size, 64)

    def gather_row(own, whole):
        me = block(yl, z, c)
        spot = whole.at[rows(me)]
        to_y = send(own, spot, yn)
        own_p, own_m = send(own, spot, zp), send(own, spot, zm)
        cores = [send(own, spot, co)]
        whole[rows(me), :] = own[...]
        yield
        to_y.wait_recv()
        spot = whole.at[rows(block(1 - yl, z, c))]
        mate_p, mate_m = send(spot, spot, zp), send(spot, spot, zm)
        cores.append(send(spot, spot, co))
        halves = []
        for y_, from_m, from_p in ((yl, own_p, own_m), (1 - yl, mate_p, mate_m)):
            from_m.wait_recv()
            b = block(y_, (z + 3) % 4, c)
            spot = whole.at[rows(b, 0, 64)]
            first = send(spot, spot, zp)
            spot = whole.at[rows(b)]
            cores.append(send(spot, spot, co))
            from_p.wait_recv()
            b = block(y_, (z + 1) % 4, c)
            spot = whole.at[rows(b, 1, 64)]
            second = send(spot, spot, zm)
            spot = whole.at[rows(b)]
            cores.append(send(spot, spot, co))
            halves.append((y_, first, second))
        yield
        for y_, first, second in halves:
            first.wait_recv()
            second.wait_recv()
            spot = whole.at[rows(block(y_, (z + 2) % 4, c))]
            cores.append(send(spot, spot, co))
        for copy in cores:
            copy.wait_recv()
        yield

    tok_steps = gather_row(tok, tok_all)
    cot_steps = gather_row(cot, cot_all)
    next(tok_steps)

    for copy in loads:
        copy.wait()
    @pl.loop(0, 8)
    def _(i):
        at = aligned(i * 128, 128)
        for j in range(7):
            cols = slice(j * 128, j * 128 + 128)
            kept_in = keep_in[i, j].astype(F32)
            w_gate[at, cols] = (w_gate[at, cols].astype(F32) * kept_in).astype(BF)
            w_up[at, cols] = (w_up[at, cols].astype(F32) * kept_in).astype(BF)

    @pl.loop(0, 7)
    def _(i):
        at = aligned(i * 128, 128)
        for j in range(8):
            cols = slice(j * 128, j * 128 + 128)
            kept_out = keep_out[i, j].astype(F32)
            w_down[at, cols] = (w_down[at, cols].astype(F32) * kept_out).astype(BF)

    next(tok_steps)
    next(cot_steps)
    next(tok_steps)
    stores = [local(tok_all, tok_hbm)]

    def tiles(body):
        @pl.loop(0, 3)
        def _(t):
            body(aligned(t * 256, 256, 256))

        body(pl.ds(768, 128))

    def product_of(lhs, rhs, transposed):
        def product(start, size, emit):
            at = aligned(start, size)

            def body(cols):
                if transposed:
                    v = lax.dot_general(
                        lhs[at, :], rhs[cols, :], (((1,), (1,)), ((), ())),
                        preferred_element_type=F32,
                    )
                else:
                    v = jnp.dot(lhs[at, :], rhs[:, cols], preferred_element_type=F32)
                emit(v, cols)
            tiles(body)
        return product

    gate_of = product_of(tok_all, w_gate, False)
    upper_of = product_of(tok_all, w_up, False)
    grad_of = product_of(cot_all, w_down, True)
    far, after, before = (x + 2) % 4, (x + 1) % 4, (x + 3) % 4

    def put(target, *terms):
        def emit(v, cols):
            for ref, at in terms:
                v = v + ref[at, cols].astype(F32)
            ref, at = target
            ref[at, cols] = v.astype(ref.dtype)
        return emit

    def reduce_x(product, s2, sp, sm, ia, ib, rp, rm, ys, yr, own):
        lo, hi, one = pl.ds(0, 256), pl.ds(256, 256), pl.ds(0, 256)
        product(far * 512, 256, put((s2, lo)))
        mid_a = send(s2.at[lo], ia, xp)
        product(far * 512 + 256, 256, put((s2, hi)))
        mid_b = send(s2.at[hi], ib, xm)
        yield
        product(after * 512 + 256, 256, put((sp, hi)))
        fin = [send(sp.at[hi], rp.at[hi], xp)]
        product(before * 512, 256, put((sm, lo)))
        fin.append(send(sm.at[lo], rm.at[lo], xm))
        yield
        mid_a.wait_recv()
        product(after * 512, 256, put((sp, lo), (ia, one)))
        fin.append(send(sp.at[lo], rp.at[lo], xp))
        mid_b.wait_recv()
        product(before * 512 + 256, 256, put((sm, hi), (ib, one)))
        fin.append(send(sm.at[hi], rm.at[hi], xm))
        yield
        for copy in fin:
            copy.wait_recv()

        def total(half, target):
            at = aligned(half * 256, 256, 256)
            product(x * 512 + half * 256, 256, put((target, one), (rp, at), (rm, at)))

        total(1 - h, ys)
        over = send(ys, yr, yh)
        total(h, own)
        yield
        over.wait_recv()
        yield

    def reduce_y(product, ys, yr, s2, sp, sm, ia, ib, rp, rm, own):
        chunks = (far, after, before, x)
        over = []
        lo, hi, one, two = pl.ds(0, 128), pl.ds(128, 128), pl.ds(0, 128), pl.ds(0, 256)

        def cross(k):
            at = pl.ds(k * 256, 256)
            product(chunks[k] * 512 + (1 - h) * 256, 256, put((ys, at)))
            over.append(send(ys.at[at], yr.at[at], yh))

        def mine(k, half):
            return chunks[k] * 512 + h * 256 + half * 128

        def came(k, half):
            return (yr, pl.ds(k * 256 + half * 128, 128))

        cross(0)
        yield
        for k in range(1, 4):
            cross(k)
        yield
        over[0].wait_recv()
        product(mine(0, 0), 256, put((s2, two), (yr, pl.ds(0, 256))))
        mid_a = send(s2.at[lo], ia, xp)
        mid_b = send(s2.at[hi], ib, xm)
        yield
        over[1].wait_recv()
        product(mine(1, 1), 128, put((sp, hi), came(1, 1)))
        fin = [send(sp.at[hi], rp.at[hi], xp)]
        yield
        over[2].wait_recv()
        product(mine(2, 0), 128, put((sm, lo), came(2, 0)))
        fin.append(send(sm.at[lo], rm.at[lo], xm))
        mid_a.wait_recv()
        product(mine(1, 0), 128, put((sp, lo), came(1, 0), (ia, one)))
        fin.append(send(sp.at[lo], rp.at[lo], xp))
        mid_b.wait_recv()
        product(mine(2, 1), 128, put((sm, hi), came(2, 1), (ib, one)))
        fin.append(send(sm.at[hi], rm.at[hi], xm))
        yield
        over[3].wait_recv()
        for copy in fin:
            copy.wait_recv()
        product(mine(3, 0), 256, put((own, two), (yr, pl.ds(768, 256)), (rp, two), (rm, two)))
        yield

    def spot_in(whole, x_, h_, part=0, size=256):
        return whole.at[aligned(x_ * 512 + h_ * 256 + part * 128, size)]

    def gather_y(own, whole, arrived=None):
        def came(x_, h_):
            if arrived is not None:
                arrived(x_, h_)

        spot = spot_in(whole, x, h)
        to_y = send(own, spot, yh)
        mine = local(own, spot)
        yield
        own_p, own_m = send(own, spot, xp), send(own, spot, xm)
        mine.wait()
        came(x, h)
        yield
        to_y.wait_recv()
        spot = spot_in(whole, x, 1 - h)
        mate_p, mate_m = send(spot, spot, xp), send(spot, spot, xm)
        came(x, 1 - h)
        yield
        halves = []
        for h_, from_m, from_p in ((h, own_p, own_m), (1 - h, mate_p, mate_m)):
            from_m.wait_recv()
            spot = spot_in(whole, before, h_, 0, 128)
            halves.append(send(spot, spot, xp))
            from_p.wait_recv()
            spot = spot_in(whole, after, h_, 1, 128)
            halves.append(send(spot, spot, xm))
            came(before, h_)
            came(after, h_)
            yield
        for i, h_ in enumerate((h, 1 - h)):
            halves[2 * i].wait_recv()
            halves[2 * i + 1].wait_recv()
            came(far, h_)
        yield

    def gather_x(own, whole):
        spot = spot_in(whole, x, h)
        own_p, own_m = send(own, spot, xp), send(own, spot, xm)
        mine = local(own, spot)
        yield
        over = [send(own, spot, yh)]
        yield
        own_p.wait_recv()
        spot = spot_in(whole, before, h, 0, 128)
        half_a = send(spot, spot, xp)
        spot = spot_in(whole, before, h)
        over.append(send(spot, spot, yh))
        own_m.wait_recv()
        spot = spot_in(whole, after, h, 1, 128)
        half_b = send(spot, spot, xm)
        spot = spot_in(whole, after, h)
        over.append(send(spot, spot, yh))
        yield
        half_a.wait_recv()
        half_b.wait_recv()
        spot = spot_in(whole, far, h)
        over.append(send(spot, spot, yh))
        yield
        for copy in over:
            copy.wait_recv()
        mine.wait()
        yield

    core = []

    def cross_core(x_, h_):
        pair = x_ * 2 + h_

        @pl.loop(0, 4)
        def _(t):
            cols = aligned(t * 256, 256, 256)
            c_s[pair, :, cols] = jnp.dot(
                hid_all[rows(pair * 2 + 1 - c), :], w_down[:, cols], preferred_element_type=F32
            )
        core.append(send(c_s.at[pair], c_r.at[pair], co))

    gate = reduce_x(gate_of, g_s2, g_sp, g_sm, g_ia, g_ib, g_rp, g_rm, g_ys, g_yr, g_own)
    upper = reduce_y(upper_of, u_ys, u_yr, u_s2, u_sp, u_sm, u_ia, u_ib, u_rp, u_rm, u_own)
    grad = reduce_x(grad_of, h_s2, h_sp, h_sm, h_ia, h_ib, h_rp, h_rm, h_ys, h_yr, h_own)
    next(gate)
    next(upper)
    next(gate)
    next(upper)
    next(cot_steps)
    next(cot_steps)
    stores.append(local(cot_all, cot_hbm))
    next(upper)
    next(gate)
    next(upper)
    next(grad)
    next(grad)
    next(upper)
    next(gate)
    next(grad)
    next(upper)
    next(gate)

    @pl.loop(0, 16)
    def _(t):
        at = aligned(t * 16, 16, 16)
        gate_v = g_own[at, :] + g_yr[at, :].astype(F32)
        upper_v = u_own[at, :]
        sigma = 1.0 / (1.0 + jnp.exp(-gate_v))
        swish = gate_v * sigma
        hid_own[at, :] = (swish * upper_v).astype(BF)
        g_own[at, :] = upper_v * sigma * (1.0 + gate_v * (1.0 - sigma))
        u_own[at, :] = swish

    hid = gather_y(hid_own, hid_all, cross_core)
    next(hid)
    next(hid)
    next(grad)
    next(hid)
    next(hid)
    next(grad)

    @pl.loop(0, 16)
    def _(t):
        at = aligned(t * 16, 16, 16)
        grad_v = h_own[at, :] + h_yr[at, :].astype(F32)
        gp_own[at, :] = (grad_v * g_own[at, :]).astype(BF)
        up_own[at, :] = (grad_v * u_own[at, :]).astype(BF)

    gp = gather_x(gp_own, gp_hbm)
    up = gather_y(up_own, up_hbm)
    next(up)
    next(gp)
    next(gp)
    next(hid)
    next(up)
    next(hid)
    next(up)
    next(gp)
    stores.append(local(hid_all, hid_hbm))

    def kept(yl_, z_):
        def piece(cols):
            part = jnp.dot(
                hid_all[rows(block(yl_, z_, c)), :], w_down[:, cols], preferred_element_type=F32
            )
            return part + c_r[yl_ * 4 + z_, :, cols]
        return piece

    def over_cols(body):
        @pl.loop(0, 4)
        def _(t):
            body(aligned(t * 256, 256, 256))

    for copy in core:
        copy.wait_recv()
    z_far, z_after, z_before = (z + 2) % 4, (z + 1) % 4, (z + 3) % 4

    def ring_piece(y_, z_, target, inc=None):
        piece = kept(y_, z_)

        def body(cols):
            v = piece(cols)
            if inc is not None:
                v = v + inc[:, cols]
            target[:, cols] = v
        over_cols(body)

    ring_piece(0, z_far, z_s2.at[0])
    z_mid_a = send(z_s2.at[0], z_i.at[0], zp)
    ring_piece(1, z_far, z_s2.at[1])
    z_mid_b = send(z_s2.at[1], z_i.at[1], zm)
    ring_piece(1, z_after, z_sp.at[1])
    z_fin = [send(z_sp.at[1], z_rp.at[1], zp)]
    ring_piece(0, z_before, z_sm.at[0])
    z_fin.append(send(z_sm.at[0], z_rm.at[0], zm))
    next(up)
    next(gp)
    z_mid_a.wait_recv()
    ring_piece(0, z_after, z_sp.at[0], z_i.at[0])
    z_fin.append(send(z_sp.at[0], z_rp.at[0], zp))
    z_mid_b.wait_recv()
    ring_piece(1, z_before, z_sm.at[1], z_i.at[1])
    z_fin.append(send(z_sm.at[1], z_rm.at[1], zm))
    next(up)
    for copy in z_fin:
        copy.wait_recv()

    def row_total(y_, target):
        piece = kept(y_, z)

        def body(cols):
            target[:, cols] = piece(cols) + z_rp[y_, :, cols] + z_rm[y_, :, cols]
        over_cols(body)

    row_total(1 - yl, o_ys)
    o_over = send(o_ys, o_yr, yn)
    row_total(yl, o_own)
    o_over.wait_recv()
    out[...] = (o_own[...] + o_yr[...]).astype(BF)
    next(up)
    next(gp)
    for copy in stores:
        copy.wait()
    for copy in sent:
        copy.wait_send()


def forward(tokens, cotangent, gate_weight, up_weight, down_weight, keep_in, keep_out):
    hbm = pl.BlockSpec(memory_space=pl.ANY)
    vmem = pl.BlockSpec(memory_space=pltpu.VMEM)

    def bf(*shape):
        return pltpu.VMEM(shape, BF)

    def f32(*shape):
        return pltpu.VMEM(shape, F32)

    def ring(n):
        return [bf(n, 896)] * 3 + [bf(n // 2, 896)] * 2 + [bf(n, 896)] * 2

    def ring_y():
        return ring(512) + [bf(256, 896), bf(256, 896), f32(256, 896)]

    smem = pl.BlockSpec(memory_space=pltpu.SMEM)
    sds = jax.ShapeDtypeStruct
    return pl.pallas_call(
        forward_kernel,
        out_shape=(
            sds((128, 1024), BF), sds((2048, 1024), BF), sds((2048, 1024), BF),
            sds((2048, 896), BF), sds((2048, 896), BF), sds((2048, 896), BF),
        ),
        in_specs=[vmem, vmem, hbm, hbm, hbm, smem, smem],
        out_specs=[vmem, hbm, hbm, hbm, hbm, hbm],
        scratch_shapes=[bf(1024, 896), bf(1024, 896), bf(896, 1024), bf(2048, 1024), bf(2048, 1024)]
        + ring_y()
        + ring_y()
        + [bf(1024, 896), bf(1024, 896)] + ring(256) + [f32(256, 896)]
        + [bf(256, 896)] * 3 + [bf(2048, 896)]
        + [f32(8, 128, 1024), f32(8, 128, 1024)]
        + [f32(2, 128, 1024)] * 6
        + [f32(128, 1024)] * 3
        + [
            pltpu.SemaphoreType.DMA((SLOTS,)), pltpu.SemaphoreType.DMA((SLOTS,)),
            pltpu.SemaphoreType.DMA((12,)),
        ],
        compiler_params=pltpu.CompilerParams(
            collective_id=0, has_side_effects=True, vmem_limit_bytes=VMEM_LIMIT
        ),
    )(tokens, cotangent, gate_weight, up_weight, down_weight, keep_in, keep_out)


def expand(mask):
    return jnp.repeat(jnp.repeat(mask, BLK, axis=0), BLK, axis=1) > 0


def shards(tokens, gate_weight, up_weight, down_weight, input_mask, output_mask, cotangent):
    output, tok_all, cot_all, hid_all, gp_all, up_all = forward(
        tokens, cotangent, gate_weight, up_weight, down_weight, input_mask, output_mask
    )
    keep_in, keep_out = expand(input_mask), expand(output_mask)
    outer = (((0,), (0,)), ((), ()))

    def grad(left, right, keep):
        full = lax.dot_general(left, right, outer, preferred_element_type=F32)
        return jnp.where(keep, full, jnp.zeros((), F32))

    grad_down = grad(hid_all, cot_all, keep_out)
    grad_gate = grad(tok_all, gp_all, keep_in)
    grad_up = grad(tok_all, up_all, keep_in)
    return (output, grad_gate, grad_up, grad_down)


def solution(mesh):
    placed = (
        P("row", "col"), P("col", "row"), P("col", "row"), P("row", "col"),
        P("col", "row"), P("row", "col"), P("row", "col"),
    )
    return jax.shard_map(
        shards, mesh=mesh, in_specs=placed,
        out_specs=(P("row", "col"), P("col", "row"), P("col", "row"), P("row", "col")),
        check_vma=False,
    )
```

time: 272 us -> 236 us (0.87)
  Pallas kernels: 240 us -> 207 us
  other arithmetic: 2.76 us -> 0.01 us
    pallas_call x1, Pallas kernels: 240 us -> 207 us  [forward(): pl.pallas_call(forward_kernel, out_shape=(sds((128, 1024), BF), sds((2048...]
where the time goes in v2:
time: 236 us
  Pallas kernels  207 us (88%)
  matrix products  22.5 us (10%)
  local copies, waits for them, and re-layouts  5.24 us (2%)
    pallas_call x1, Pallas kernels, forward(): pl.pallas_call(forward_kernel, out_shape=(sds((128, 1024), BF), sds((2048...  207 us
    dot_general x3, matrix products, grad(): full = lax.dot_general(left, right, outer, preferred_element_type=F32)  22.5 us

profile of v2, /device:TPU:0, one launch (start us, length us, event | category | flops | bytes accessed | tf_op | source)
XLA Modules:
  0.0 235.6 jit_solution(2053416911673148681)
XLA Ops:
  0.6 0.0 copy-start.1
  0.6 207.1 %shard_map.102 = (bf16[128,1024]{1,0:T(8,128)(2,1)}, bf16[2048,1024]{1,0:T(8,128)(2,1)}, bf16[2048,1024]{1,0:T(8,128)(2,1)}, bf16[2048,896]{1,0:T(8,128)(2,1)}, ...) custom-call(bf16[128,1024]{1,0:T(8,128)(2,1)} %tok.1, bf16[128,1024]{1,0:T(8,128)(2,1)} %cot.1, ...), custom_call_target="tpu_custom_call" | custom-call | tf_op jit(solution)/shard_map/pallas_call | solution.py:486
  207.8 0.0 copy-done.1
  207.8 0.1 copy.11
  207.9 0.1 broadcast_bitcast_fusion
  208.0 0.2 broadcast_in_dim.22
  208.2 1.0 copy.12
  209.3 0.0 copy-start.4
  209.3 0.0 copy-start.6
  209.3 9.9 %broadcast_select_fusion = f32[1024,896]{1,0:T(8,128)} fusion(pred[1024,896]{1,0:T(32,128)(4,1)S(1)} %copy.12, bf16[2048,1024]{1,0:T(8,128)(2,1)} %get-tuple-element.11, bf16[2048,896]{1,0:T(8,128)(2,1)} %get-tuple-element.13), kind=kOutput, calls=%fused_computation.1 | convolution fusion | flops 3759013888 | bytes 12451840 | tf_op jit(solution)/shard_map/dot_general | solution.py:524
  219.2 0.0 copy-done.4
  219.2 0.0 copy-done.6
  219.2 0.0 copy-start.2
  219.2 0.0 copy-start.3
  219.2 0.0 copy-start.5
  219.2 6.6 %broadcast_select_fusion.1 = f32[1024,896]{1,0:T(8,128)} fusion(pred[1024,896]{1,0:T(32,128)(4,1)S(1)} %copy.12, bf16[2048,1024]{1,0:T(8,128)(2,1)S(1)} %copy-done.4, bf16[2048,896]{1,0:T(8,128)(2,1)S(1)} %copy-done.6), kind=kOutput, calls=%fused_computation.2 | convolution fusion | flops 3759013888 | bytes 12451840 | tf_op jit(solution)/shard_map/dot_general | solution.py:524
  225.8 0.0 copy-done.2
  225.8 3.0 %broadcast_in_dim.25 = pred[896,8,128]{2,1,0:T(8,128)(4,1)S(1)} broadcast(pred[896,8]{1,0:T(8,128)(4,1)S(1)} %bitcast.20), dimensions={0,1} | broadcast | bytes 924672 | tf_op jit(solution)/shard_map/broadcast_in_dim | solution.py:513
  228.8 0.0 copy-done.3
  228.8 0.0 copy-done.5
  228.8 0.0 copy-start
  228.9 6.1 %bitcast_select_fusion = f32[896,1024]{1,0:T(8,128)} fusion(pred[112,8,8,128]{3,2,1,0:T(8,128)(4,1)S(1)} %bitcast.19, bf16[2048,896]{1,0:T(8,128)(2,1)S(1)} %copy-done.5, bf16[2048,1024]{1,0:T(8,128)(2,1)S(1)} %copy-done.3), kind=kOutput, calls=%fused_computation | convolution fusion | flops 3759013888 | bytes 12451840 | tf_op jit(solution)/shard_map/dot_general | solution.py:524
  234.9 0.0 copy-done
  234.9 0.7 copy.22
  (4 shorter events, 0.1 us)
Async XLA Ops:
  0.6 207.1 %copy-start.1 = (s32[8,7]{1,0:T(8,128)S(1)}, s32[8,7]{1,0:T(8,128)}, u32[]{:S(2)}) copy-start(s32[8,7]{1,0:T(8,128)} %keep_in.1) | copy-start | bytes 676
  209.3 9.9 %copy-start.4 = (bf16[2048,1024]{1,0:T(8,128)(2,1)S(1)}, bf16[2048,1024]{1,0:T(8,128)(2,1)}, u32[]{:S(2)}) copy-start(bf16[2048,1024]{1,0:T(8,128)(2,1)} %get-tuple-element.11) | copy-start | bytes 12582916
  209.3 9.9 %copy-start.6 = (bf16[2048,896]{1,0:T(8,128)(2,1)S(1)}, bf16[2048,896]{1,0:T(8,128)(2,1)}, u32[]{:S(2)}) copy-start(bf16[2048,896]{1,0:T(8,128)(2,1)} %get-tuple-element.12) | copy-start | bytes 11010052
  219.2 6.6 %copy-start.2 = (s32[7,8]{1,0:T(8,128)S(1)}, s32[7,8]{1,0:T(8,128)}, u32[]{:S(2)}) copy-start(s32[7,8]{1,0:T(8,128)} %keep_out.1) | copy-start | bytes 676
  219.2 9.7 %copy-start.3 = (bf16[2048,1024]{1,0:T(8,128)(2,1)S(1)}, bf16[2048,1024]{1,0:T(8,128)(2,1)}, u32[]{:S(2)}) copy-start(bf16[2048,1024]{1,0:T(8,128)(2,1)} %get-tuple-element.15) | copy-start | bytes 12582916
  219.2 9.7 %copy-start.5 = (bf16[2048,896]{1,0:T(8,128)(2,1)S(1)}, bf16[2048,896]{1,0:T(8,128)(2,1)}, u32[]{:S(2)}) copy-start(bf16[2048,896]{1,0:T(8,128)(2,1)} %get-tuple-element.14) | copy-start | bytes 11010052
  228.8 6.1 %copy-start = (bf16[128,1024]{1,0:T(8,128)(2,1)S(1)}, bf16[128,1024]{1,0:T(8,128)(2,1)}, u32[]{:S(2)}) copy-start(bf16[128,1024]{1,0:T(8,128)(2,1)} %get-tuple-element.20) | copy-start | bytes 786436

commit v3 on v2

--- a/solution.py
+++ b/solution.py
@@ -5,7 +5,6 @@
 from jax.experimental.pallas import tpu as pltpu
 from jax.sharding import PartitionSpec as P
 
-BLK = 128
 BF = jnp.bfloat16
 F32 = jnp.float32
 MESH = pl.DeviceIdType.MESH
@@ -19,13 +18,13 @@
 
 def forward_kernel(
     tok, cot, gate_w, up_w, down_w, keep_in, keep_out,
-    out, tok_hbm, cot_hbm, hid_hbm, gp_hbm, up_hbm,
+    out, tok_t_hbm, down_hbm, gp_hbm, up_hbm,
     w_gate, w_up, w_down, tok_all, cot_all,
     g_s2, g_sp, g_sm, g_ia, g_ib, g_rp, g_rm, g_ys, g_yr, g_own,
     h_s2, h_sp, h_sm, h_ia, h_ib, h_rp, h_rm, h_ys, h_yr, h_own,
     u_ys, u_yr, u_s2, u_sp, u_sm, u_ia, u_ib, u_rp, u_rm, u_own,
     hid_own, gp_own, up_own, hid_all,
-    c_s, c_r, z_s2, z_i, z_sp, z_sm, z_rp, z_rm, o_ys, o_yr, o_own,
+    c_s, c_r, z_s2, z_i, z_sp, z_sm, z_rp, z_rm, o_ys, o_yr, o_own, tok_t, down_t,
     send_sem, recv_sem, local_sem,
 ):
     row = lax.axis_index("row")
@@ -143,7 +142,33 @@
     next(tok_steps)
     next(cot_steps)
     next(tok_steps)
-    stores = [local(tok_all, tok_hbm)]
+    flips = []
+
+    def flip(first, last):
+        for i in range(first, last):
+            if len(flips) >= 2:
+                flips[-2].wait()
+            at = slice(i * 128, i * 128 + 128)
+            tok_t[i % 2] = tok_all[:, at].T
+            flips.append(local(tok_t.at[i % 2], tok_t_hbm.at[at]))
+
+    downs = []
+
+    def down_grad(i):
+        if len(downs) >= 2:
+            downs[-2].wait()
+        units = slice(i * 128, i * 128 + 128)
+        left = hid_all[:, units].T
+
+        @pl.loop(0, 4)
+        def _(t):
+            v = jnp.dot(left, cot_all[:, aligned(t * 256, 256, 256)], preferred_element_type=F32)
+            for j in range(2):
+                kept_out = keep_out[i, 2 * t + j].astype(F32)
+                down_t[i % 2, :, aligned(t * 256 + j * 128, 128)] = (
+                    v[:, j * 128 : j * 128 + 128] * kept_out
+                )
+        downs.append(local(down_t.at[i % 2], down_hbm.at[units]))
 
     def tiles(body):
         @pl.loop(0, 3)
@@ -347,15 +372,18 @@
     next(gate)
     next(upper)
     next(cot_steps)
+    flip(0, 2)
     next(cot_steps)
-    stores.append(local(cot_all, cot_hbm))
     next(upper)
     next(gate)
     next(upper)
     next(grad)
     next(grad)
+    flip(2, 4)
     next(upper)
+    flip(4, 6)
     next(gate)
+    flip(6, 8)
     next(grad)
     next(upper)
     next(gate)
@@ -396,7 +424,6 @@
     next(hid)
     next(up)
     next(gp)
-    stores.append(local(hid_all, hid_hbm))
 
     def kept(yl_, z_):
         def piece(cols):
@@ -411,6 +438,7 @@
         def _(t):
             body(aligned(t * 256, 256, 256))
 
+    down_grad(0)
     for copy in core:
         copy.wait_recv()
     z_far, z_after, z_before = (z + 2) % 4, (z + 1) % 4, (z + 3) % 4
@@ -435,13 +463,19 @@
     z_fin.append(send(z_sm.at[0], z_rm.at[0], zm))
     next(up)
     next(gp)
+    down_grad(1)
+    down_grad(2)
     z_mid_a.wait_recv()
     ring_piece(0, z_after, z_sp.at[0], z_i.at[0])
     z_fin.append(send(z_sp.at[0], z_rp.at[0], zp))
     z_mid_b.wait_recv()
     ring_piece(1, z_before, z_sm.at[1], z_i.at[1])
     z_fin.append(send(z_sm.at[1], z_rm.at[1], zm))
+    down_grad(3)
+    down_grad(4)
     next(up)
+    down_grad(5)
+    down_grad(6)
     for copy in z_fin:
         copy.wait_recv()
 
@@ -459,7 +493,7 @@
     out[...] = (o_own[...] + o_yr[...]).astype(BF)
     next(up)
     next(gp)
-    for copy in stores:
+    for copy in flips[-2:] + downs[-2:]:
         copy.wait()
     for copy in sent:
         copy.wait_send()
@@ -486,11 +520,11 @@
     return pl.pallas_call(
         forward_kernel,
         out_shape=(
-            sds((128, 1024), BF), sds((2048, 1024), BF), sds((2048, 1024), BF),
-            sds((2048, 896), BF), sds((2048, 896), BF), sds((2048, 896), BF),
+            sds((128, 1024), BF), sds((1024, 2048), BF), sds((896, 1024), F32),
+            sds((2048, 896), BF), sds((2048, 896), BF),
         ),
         in_specs=[vmem, vmem, hbm, hbm, hbm, smem, smem],
-        out_specs=[vmem, hbm, hbm, hbm, hbm, hbm],
+        out_specs=[vmem, hbm, hbm, hbm, hbm],
         scratch_shapes=[bf(1024, 896), bf(1024, 896), bf(896, 1024), bf(2048, 1024), bf(2048, 1024)]
         + ring_y()
         + ring_y()
@@ -499,9 +533,10 @@
         + [f32(8, 128, 1024), f32(8, 128, 1024)]
         + [f32(2, 128, 1024)] * 6
         + [f32(128, 1024)] * 3
+        + [bf(2, 128, 2048), f32(2, 128, 1024)]
         + [
             pltpu.SemaphoreType.DMA((SLOTS,)), pltpu.SemaphoreType.DMA((SLOTS,)),
-            pltpu.SemaphoreType.DMA((12,)),
+            pltpu.SemaphoreType.DMA((24,)),
         ],
         compiler_params=pltpu.CompilerParams(
             collective_id=0, has_side_effects=True, vmem_limit_bytes=VMEM_LIMIT
@@ -509,24 +544,51 @@
     )(tokens, cotangent, gate_weight, up_weight, down_weight, keep_in, keep_out)
 
 
-def expand(mask):
-    return jnp.repeat(jnp.repeat(mask, BLK, axis=0), BLK, axis=1) > 0
+def input_grads_kernel(keep_in, tok_t, gp, up, gate_out, up_out):
+    i = pl.program_id(0)
+
+    def one(grads, target):
+        def tile(cols, blocks, first):
+            v = jnp.dot(tok_t[...], grads[:, cols], preferred_element_type=F32)
+            for a in range(2):
+                for b in range(blocks):
+                    kept_in = keep_in[2 * i + a, first + b].astype(F32)
+                    at = slice(a * 128, a * 128 + 128)
+                    target[at, (first + b) * 128 : (first + b) * 128 + 128] = (
+                        v[at, b * 128 : b * 128 + 128] * kept_in
+                    )
+        for t in range(3):
+            tile(slice(t * 256, t * 256 + 256), 2, 2 * t)
+        tile(slice(768, 896), 1, 6)
+
+    one(gp, gate_out)
+    one(up, up_out)
+
+
+def input_grads(keep_in, tok_t, gp, up):
+    whole = pl.BlockSpec((2048, 896), lambda i: (0, 0), pipeline_mode=pl.Buffered(1))
+    piece = pl.BlockSpec((256, 896), lambda i: (i, 0))
+    return pl.pallas_call(
+        input_grads_kernel,
+        grid=(4,),
+        out_shape=(jax.ShapeDtypeStruct((1024, 896), F32),) * 2,
+        in_specs=[
+            pl.BlockSpec(memory_space=pltpu.SMEM),
+            pl.BlockSpec((256, 2048), lambda i: (i, 0)), whole, whole,
+        ],
+        out_specs=[piece, piece],
+        compiler_params=pltpu.CompilerParams(vmem_limit_bytes=40 * 2**20),
+        cost_estimate=pl.CostEstimate(
+            flops=4 * 2048 * 1024 * 896, bytes_accessed=20 * 2**20, transcendentals=0
+        ),
+    )(keep_in, tok_t, gp, up)
 
 
 def shards(tokens, gate_weight, up_weight, down_weight, input_mask, output_mask, cotangent):
-    output, tok_all, cot_all, hid_all, gp_all, up_all = forward(
+    output, tok_t, grad_down, gp, up = forward(
         tokens, cotangent, gate_weight, up_weight, down_weight, input_mask, output_mask
     )
-    keep_in, keep_out = expand(input_mask), expand(output_mask)
-    outer = (((0,), (0,)), ((), ()))
-
-    def grad(left, right, keep):
-        full = lax.dot_general(left, right, outer, preferred_element_type=F32)
-        return jnp.where(keep, full, jnp.zeros((), F32))
-
-    grad_down = grad(hid_all, cot_all, keep_out)
-    grad_gate = grad(tok_all, gp_all, keep_in)
-    grad_up = grad(tok_all, up_all, keep_in)
+    grad_gate, grad_up = input_grads(input_mask, tok_t, gp, up)
     return (output, grad_gate, grad_up, grad_down)
 
 

time: 236 us -> 229 us (0.970)
  matrix products: 22.5 us -> 0 us
  Pallas kernels: 207 us -> 219 us
  local copies, waits for them, and re-layouts: 5.24 us -> 8.81 us
    dot_general x3 -> x0, matrix products: 22.5 us -> none  [grad(): full = lax.dot_general(left, right, outer, preferred_element_type=F32)]
    pallas_call x1 -> x2, Pallas kernels: 207 us -> 219 us  [the longest x1 208 us: forward(): pl.pallas_call(forward_kernel, out_shape=(sds((128, 1024), BF), sds((1024...]
    unnamed x17 -> x14, local copies, waits for them, and re-layouts: 0.82 us -> 8.81 us
    broadcast_in_dim x3 -> x0, local copies, waits for them, and re-layouts: 3.29 us -> none  [expand(): return jnp.repeat(jnp.repeat(mask, BLK, axis=0), BLK, axis=1) > 0]
where the time goes in v3:
time: 229 us; the launch traced here: 228 us
  Pallas kernels  219 us (96%)
  local copies, waits for them, and re-layouts  8.81 us (4%)
    pallas_call x1, Pallas kernels, forward(): pl.pallas_call(forward_kernel, out_shape=(sds((128, 1024), BF), sds((1024...  208 us
    pallas_call x1, Pallas kernels, input_grads(): pl.pallas_call(input_grads_kernel, grid=(4,), out_shape=(jax.ShapeDtypeSt...  11.1 us
    unnamed x14, local copies, waits for them, and re-layouts  8.81 us

profile of v3, /device:TPU:0, one launch (start us, length us, event | category | flops | bytes accessed | tf_op | source)
XLA Modules:
  0.0 228.3 jit_solution(8681442284269230222)
XLA Ops:
  0.6 0.0 copy-start
  0.6 207.7 %shard_map.102 = (bf16[128,1024]{1,0:T(8,128)(2,1)}, bf16[1024,2048]{1,0:T(8,128)(2,1)}, f32[896,1024]{1,0:T(8,128)}, bf16[2048,896]{1,0:T(8,128)(2,1)}, bf16[2048,896]{1,0:T(8,128)(2,1)}) custom-call(bf16[128,1024]{1,0:T(8,128)(2,1)} %tok.1, bf16[128,1024]{1,0:T(8,128)(2,1)} %cot.1, bf16[1024,896]{1,0:T(8,128)(2,1)} %gate_w.1, bf16[1024,896]{1,0:T(8,128)(2,1)} %up_w.1, ...), custom_call_target="tpu_custom_call" | custom-call | tf_op jit(solution)/shard_map/pallas_call | solution.py:520
  208.3 0.0 copy-done
  208.3 0.0 copy-start.1
  208.3 2.2 copy-done.1
  210.5 0.0 copy-start.2
  210.5 2.0 copy-done.2
  212.6 0.0 copy-start.3
  212.6 2.0 copy-done.3
  214.6 0.0 copy-start.5
  214.6 0.0 copy-start.4
  214.6 11.1 %shard_map.103 = (f32[1024,896]{1,0:T(8,128)}, f32[1024,896]{1,0:T(8,128)}) custom-call(s32[8,7]{1,0:T(8,128)S(1)} %copy-done, bf16[1024,2048]{1,0:T(8,128)(2,1)S(1)} %copy-done.1, bf16[2048,896]{1,0:T(8,128)(2,1)S(1)} %copy-done.2, bf16[2048,896]{1,0:T(8,128)(2,1)S(1)} %copy-done.3), custom_call_target="tpu_custom_call" | custom-call | flops 7516192768 | bytes 20971520 | tf_op jit(solution)/shard_map/pallas_call | solution.py:571
  225.7 0.0 copy-done.5
  225.7 0.7 copy.13
  226.4 0.0 copy-done.4
  226.4 1.8 copy.14
Async XLA Ops:
  0.6 207.7 %copy-start = (s32[8,7]{1,0:T(8,128)S(1)}, s32[8,7]{1,0:T(8,128)}, u32[]{:S(2)}) copy-start(s32[8,7]{1,0:T(8,128)} %keep_in.3) | copy-start | bytes 676
  208.3 2.2 copy-start.1
  210.5 2.0 copy-start.2
  212.6 2.0 copy-start.3
  214.6 11.1 %copy-start.5 = (bf16[128,1024]{1,0:T(8,128)(2,1)S(1)}, bf16[128,1024]{1,0:T(8,128)(2,1)}, u32[]{:S(2)}) copy-start(bf16[128,1024]{1,0:T(8,128)(2,1)} %get-tuple-element.22) | copy-start | bytes 786436
  214.6 11.8 %copy-start.4 = (f32[896,1024]{1,0:T(8,128)S(1)}, f32[896,1024]{1,0:T(8,128)}, u32[]{:S(2)}) copy-start(f32[896,1024]{1,0:T(8,128)} %get-tuple-element.25) | copy-start | bytes 11010052

commit v4 on v3

--- a/solution.py
+++ b/solution.py
@@ -544,8 +544,16 @@
     )(tokens, cotangent, gate_weight, up_weight, down_weight, keep_in, keep_out)
 
 
-def input_grads_kernel(keep_in, tok_t, gp, up, gate_out, up_out):
+def input_grads_kernel(keep_in, tok_t, gp_hbm, up_hbm, gate_out, up_out, gp, up, sems):
     i = pl.program_id(0)
+    gp_load = pltpu.make_async_copy(gp_hbm, gp, sems.at[0])
+    up_load = pltpu.make_async_copy(up_hbm, up, sems.at[1])
+
+    @pl.when(i == 0)
+    def _():
+        gp_load.start()
+        up_load.start()
+        gp_load.wait()
 
     def one(grads, target):
         def tile(cols, blocks, first):
@@ -562,11 +570,16 @@
         tile(slice(768, 896), 1, 6)
 
     one(gp, gate_out)
+
+    @pl.when(i == 0)
+    def _():
+        up_load.wait()
+
     one(up, up_out)
 
 
 def input_grads(keep_in, tok_t, gp, up):
-    whole = pl.BlockSpec((2048, 896), lambda i: (0, 0), pipeline_mode=pl.Buffered(1))
+    whole = pl.BlockSpec(memory_space=pl.ANY)
     piece = pl.BlockSpec((256, 896), lambda i: (i, 0))
     return pl.pallas_call(
         input_grads_kernel,
@@ -577,7 +590,10 @@
             pl.BlockSpec((256, 2048), lambda i: (i, 0)), whole, whole,
         ],
         out_specs=[piece, piece],
-        compiler_params=pltpu.CompilerParams(vmem_limit_bytes=40 * 2**20),
+        scratch_shapes=[
+            pltpu.VMEM((2048, 896), BF), pltpu.VMEM((2048, 896), BF), pltpu.SemaphoreType.DMA((2,)),
+        ],
+        compiler_params=pltpu.CompilerParams(vmem_limit_bytes=VMEM_LIMIT),
         cost_estimate=pl.CostEstimate(
             flops=4 * 2048 * 1024 * 896, bytes_accessed=20 * 2**20, transcendentals=0
         ),

time: 229 us -> 228 us (level)
  local copies, waits for them, and re-layouts: 8.81 us -> 5.08 us
  Pallas kernels: 219 us -> 222 us
    unnamed x14 -> x4, local copies, waits for them, and re-layouts: 8.81 us -> 5.08 us
    pallas_call x1, Pallas kernels: 11.1 us -> 14.7 us  [input_grads(): pl.pallas_call(input_grads_kernel, grid=(4,), out_shape=(jax.ShapeDtypeSt...]
where the time goes in v4:
time: 228 us
  Pallas kernels  222 us (97%)
  local copies, waits for them, and re-layouts  5.08 us (2%)
    pallas_call x1, Pallas kernels, forward(): pl.pallas_call(forward_kernel, out_shape=(sds((128, 1024), BF), sds((1024...  208 us
    pallas_call x1, Pallas kernels, input_grads(): pl.pallas_call(input_grads_kernel, grid=(4,), out_shape=(jax.ShapeDtypeSt...  14.7 us
    unnamed x4, local copies, waits for them, and re-layouts  5.08 us

profile of v4, /device:TPU:0, one launch (start us, length us, event | category | flops | bytes accessed | tf_op | source)
XLA Modules:
  0.0 228.1 jit_solution(237193599196727962)
XLA Ops:
  0.6 207.7 %shard_map.102 = (bf16[128,1024]{1,0:T(8,128)(2,1)}, bf16[1024,2048]{1,0:T(8,128)(2,1)}, f32[896,1024]{1,0:T(8,128)}, bf16[2048,896]{1,0:T(8,128)(2,1)}, bf16[2048,896]{1,0:T(8,128)(2,1)}) custom-call(bf16[128,1024]{1,0:T(8,128)(2,1)} %tok.1, bf16[128,1024]{1,0:T(8,128)(2,1)} %cot.1, bf16[1024,896]{1,0:T(8,128)(2,1)} %gate_w.1, bf16[1024,896]{1,0:T(8,128)(2,1)} %up_w.1, ...), custom_call_target="tpu_custom_call" | custom-call | tf_op jit(solution)/shard_map/pallas_call | solution.py:520
  208.3 0.0 copy-start
  208.3 14.7 %shard_map.103 = (f32[1024,896]{1,0:T(8,128)}, f32[1024,896]{1,0:T(8,128)}) custom-call(s32[8,7]{1,0:T(8,128)} %keep_in.3, bf16[1024,2048]{1,0:T(8,128)(2,1)} %get-tuple-element.12.tok_t, bf16[2048,896]{1,0:T(8,128)(2,1)} %get-tuple-element.13.gp_hbm, bf16[2048,896]{1,0:T(8,128)(2,1)} %get-tuple-element.14.up_hbm), custom_call_target="tpu_custom_call" | custom-call | flops 7516192768 | bytes 20971520 | tf_op jit(solution)/shard_map/pallas_call | solution.py:584
  223.0 0.0 copy-done
  223.0 0.7 copy.13
  223.7 4.4 %copy.14 = f32[896,1024]{1,0:T(8,128)} copy(f32[896,1024]{1,0:T(8,128)} %get-tuple-element.25) | data formatting | bytes 7340032
Async XLA Ops:
  208.3 14.7 %copy-start = (bf16[128,1024]{1,0:T(8,128)(2,1)S(1)}, bf16[128,1024]{1,0:T(8,128)(2,1)}, u32[]{:S(2)}) copy-start(bf16[128,1024]{1,0:T(8,128)(2,1)} %get-tuple-element.22) | copy-start | bytes 786436

commit v5 on v3

--- a/solution.py
+++ b/solution.py
@@ -544,51 +544,93 @@
     )(tokens, cotangent, gate_weight, up_weight, down_weight, keep_in, keep_out)
 
 
-def input_grads_kernel(keep_in, tok_t, gp, up, gate_out, up_out):
-    i = pl.program_id(0)
-
-    def one(grads, target):
-        def tile(cols, blocks, first):
-            v = jnp.dot(tok_t[...], grads[:, cols], preferred_element_type=F32)
-            for a in range(2):
-                for b in range(blocks):
-                    kept_in = keep_in[2 * i + a, first + b].astype(F32)
-                    at = slice(a * 128, a * 128 + 128)
-                    target[at, (first + b) * 128 : (first + b) * 128 + 128] = (
-                        v[at, b * 128 : b * 128 + 128] * kept_in
+def input_grads_kernel(
+    keep_in, tok_t_hbm, gp_hbm, up_hbm, down_hbm, out_hbm,
+    gate_grad, up_grad, down_grad, output, tok_t, gp, up, down, out, done, sems,
+):
+    lo, hi = slice(0, 512), slice(512, 1024)
+    moves = (
+        (tok_t_hbm.at[lo], tok_t.at[lo]), (gp_hbm, gp), (up_hbm, up),
+        (tok_t_hbm.at[hi], tok_t.at[hi]), (down_hbm, down), (out_hbm, out),
+    )
+    loads = [pltpu.make_async_copy(src, dst, sems.at[i]) for i, (src, dst) in enumerate(moves)]
+    for load in loads:
+        load.start()
+    stores = []
+
+    def part(half, grads, target):
+        k = len(stores)
+        if k >= 2:
+            stores[k - 2].wait()
+        at = slice(half * 512, half * 512 + 512)
+        buf = done.at[k % 2]
+
+        def tile(start, first, blocks):
+            v = jnp.dot(
+                tok_t[at, :], grads[:, aligned(start, blocks * 128)], preferred_element_type=F32
+            )
+            for i in range(4):
+                for j in range(blocks):
+                    kept_in = keep_in[half * 4 + i, first + j].astype(F32)
+                    buf[i * 128 : i * 128 + 128, aligned(start + j * 128, 128)] = (
+                        v[i * 128 : i * 128 + 128, j * 128 : j * 128 + 128] * kept_in
                     )
-        for t in range(3):
-            tile(slice(t * 256, t * 256 + 256), 2, 2 * t)
-        tile(slice(768, 896), 1, 6)
-
-    one(gp, gate_out)
-    one(up, up_out)
-
-
-def input_grads(keep_in, tok_t, gp, up):
-    whole = pl.BlockSpec((2048, 896), lambda i: (0, 0), pipeline_mode=pl.Buffered(1))
-    piece = pl.BlockSpec((256, 896), lambda i: (i, 0))
+
+        @pl.loop(0, 3)
+        def _(t):
+            tile(t * 256, 2 * t, 2)
+
+        tile(768, 6, 1)
+        store = pltpu.make_async_copy(buf, target.at[at], sems.at[6 + k])
+        store.start()
+        stores.append(store)
+
+    loads[0].wait()
+    loads[1].wait()
+    part(0, gp, gate_grad)
+    loads[2].wait()
+    part(0, up, up_grad)
+    loads[3].wait()
+    loads[4].wait()
+    loads[5].wait()
+    passed = [
+        pltpu.make_async_copy(down, down_grad, sems.at[10]),
+        pltpu.make_async_copy(out, output, sems.at[11]),
+    ]
+    for copy in passed:
+        copy.start()
+    part(1, gp, gate_grad)
+    part(1, up, up_grad)
+    for copy in passed + stores[2:]:
+        copy.wait()
+
+
+def input_grads(keep_in, tok_t, gp, up, down, out):
+    hbm = pl.BlockSpec(memory_space=pl.ANY)
+    sds = jax.ShapeDtypeStruct
     return pl.pallas_call(
         input_grads_kernel,
-        grid=(4,),
-        out_shape=(jax.ShapeDtypeStruct((1024, 896), F32),) * 2,
-        in_specs=[
-            pl.BlockSpec(memory_space=pltpu.SMEM),
-            pl.BlockSpec((256, 2048), lambda i: (i, 0)), whole, whole,
+        out_shape=(
+            sds((1024, 896), F32), sds((1024, 896), F32), sds((896, 1024), F32),
+            sds((128, 1024), BF),
+        ),
+        in_specs=[pl.BlockSpec(memory_space=pltpu.SMEM)] + [hbm] * 5,
+        out_specs=[hbm] * 4,
+        scratch_shapes=[
+            pltpu.VMEM((1024, 2048), BF), pltpu.VMEM((2048, 896), BF),
+            pltpu.VMEM((2048, 896), BF), pltpu.VMEM((896, 1024), F32),
+            pltpu.VMEM((128, 1024), BF), pltpu.VMEM((2, 512, 896), F32),
+            pltpu.SemaphoreType.DMA((12,)),
         ],
-        out_specs=[piece, piece],
-        compiler_params=pltpu.CompilerParams(vmem_limit_bytes=40 * 2**20),
-        cost_estimate=pl.CostEstimate(
-            flops=4 * 2048 * 1024 * 896, bytes_accessed=20 * 2**20, transcendentals=0
-        ),
-    )(keep_in, tok_t, gp, up)
+        compiler_params=pltpu.CompilerParams(vmem_limit_bytes=VMEM_LIMIT),
+    )(keep_in, tok_t, gp, up, down, out)
 
 
 def shards(tokens, gate_weight, up_weight, down_weight, input_mask, output_mask, cotangent):
-    output, tok_t, grad_down, gp, up = forward(
+    out, tok_t, down, gp, up = forward(
         tokens, cotangent, gate_weight, up_weight, down_weight, input_mask, output_mask
     )
-    grad_gate, grad_up = input_grads(input_mask, tok_t, gp, up)
+    grad_gate, grad_up, grad_down, output = input_grads(input_mask, tok_t, gp, up, down, out)
     return (output, grad_gate, grad_up, grad_down)
 
 

time: 229 us -> 225 us (0.983)
  local copies, waits for them, and re-layouts: 8.81 us -> 0 us
  Pallas kernels: 219 us -> 224 us
    unnamed x14 -> x0, local copies, waits for them, and re-layouts: 8.81 us -> none
    pallas_call x1, Pallas kernels: 11.1 us -> 16.2 us  [input_grads(): pl.pallas_call(input_grads_kernel, out_shape=(sds((1024, 896), F32), sds(...]
where the time goes in v5:
time: 225 us
  Pallas kernels  224 us (100%)
    pallas_call x1, Pallas kernels, forward(): pl.pallas_call(forward_kernel, out_shape=(sds((128, 1024), BF), sds((1024...  208 us
    pallas_call x1, Pallas kernels, input_grads(): pl.pallas_call(input_grads_kernel, out_shape=(sds((1024, 896), F32), sds(...  16.2 us

profile of v5, /device:TPU:0, one launch (start us, length us, event | category | flops | bytes accessed | tf_op | source)
XLA Modules:
  0.0 224.7 jit_solution(9507047333336605558)
XLA Ops:
  0.6 207.7 %shard_map.102 = (bf16[128,1024]{1,0:T(8,128)(2,1)}, bf16[1024,2048]{1,0:T(8,128)(2,1)}, f32[896,1024]{1,0:T(8,128)}, bf16[2048,896]{1,0:T(8,128)(2,1)}, bf16[2048,896]{1,0:T(8,128)(2,1)}) custom-call(bf16[128,1024]{1,0:T(8,128)(2,1)} %tok.1, bf16[128,1024]{1,0:T(8,128)(2,1)} %cot.1, bf16[1024,896]{1,0:T(8,128)(2,1)} %gate_w.1, bf16[1024,896]{1,0:T(8,128)(2,1)} %up_w.1, ...), custom_call_target="tpu_custom_call" | custom-call | tf_op jit(solution)/shard_map/pallas_call | solution.py:520
  208.3 16.2 %shard_map.103 = (f32[1024,896]{1,0:T(8,128)}, f32[1024,896]{1,0:T(8,128)}, f32[896,1024]{1,0:T(8,128)}, bf16[128,1024]{1,0:T(8,128)(2,1)}) custom-call(s32[8,7]{1,0:T(8,128)} %keep_in.3, bf16[1024,2048]{1,0:T(8,128)(2,1)} %get-tuple-element.13.tok_t_hbm, bf16[2048,896]{1,0:T(8,128)(2,1)} %get-tuple-element.14.gp_hbm, ...), custom_call_target="tpu_custom_call" | custom-call | tf_op jit(solution)/shard_map/pallas_call | solution.py:611

commit v6 on v5

--- a/solution.py
+++ b/solution.py
@@ -10,6 +10,7 @@
 MESH = pl.DeviceIdType.MESH
 VMEM_LIMIT = 62 * 2**20
 SLOTS = 112
+K2_ROWS = 256
 
 
 def aligned(start, size, to=128):
@@ -483,14 +484,15 @@
         piece = kept(y_, z)
 
         def body(cols):
-            target[:, cols] = piece(cols) + z_rp[y_, :, cols] + z_rm[y_, :, cols]
+            total = piece(cols) + z_rp[y_, :, cols] + z_rm[y_, :, cols]
+            target[:, cols] = total.astype(target.dtype)
         over_cols(body)
 
     row_total(1 - yl, o_ys)
     o_over = send(o_ys, o_yr, yn)
     row_total(yl, o_own)
     o_over.wait_recv()
-    out[...] = (o_own[...] + o_yr[...]).astype(BF)
+    out[...] = (o_own[...] + o_yr[...].astype(F32)).astype(BF)
     next(up)
     next(gp)
     for copy in flips[-2:] + downs[-2:]:
@@ -532,7 +534,7 @@
         + [bf(256, 896)] * 3 + [bf(2048, 896)]
         + [f32(8, 128, 1024), f32(8, 128, 1024)]
         + [f32(2, 128, 1024)] * 6
-        + [f32(128, 1024)] * 3
+        + [bf(128, 1024), bf(128, 1024), f32(128, 1024)]
         + [bf(2, 128, 2048), f32(2, 128, 1024)]
         + [
             pltpu.SemaphoreType.DMA((SLOTS,)), pltpu.SemaphoreType.DMA((SLOTS,)),
@@ -554,7 +556,7 @@
         (tok_t_hbm.at[hi], tok_t.at[hi]), (down_hbm, down), (out_hbm, out),
     )
     loads = [pltpu.make_async_copy(src, dst, sems.at[i]) for i, (src, dst) in enumerate(moves)]
-    for load in loads:
+    for load in loads[:2]:
         load.start()
     stores = []
 
@@ -566,15 +568,19 @@
         buf = done.at[k % 2]
 
         def tile(start, first, blocks):
-            v = jnp.dot(
-                tok_t[at, :], grads[:, aligned(start, blocks * 128)], preferred_element_type=F32
-            )
-            for i in range(4):
-                for j in range(blocks):
-                    kept_in = keep_in[half * 4 + i, first + j].astype(F32)
-                    buf[i * 128 : i * 128 + 128, aligned(start + j * 128, 128)] = (
-                        v[i * 128 : i * 128 + 128, j * 128 : j * 128 + 128] * kept_in
-                    )
+            for r in range(512 // K2_ROWS):
+                some = slice(half * 512 + r * K2_ROWS, half * 512 + (r + 1) * K2_ROWS)
+                v = jnp.dot(
+                    tok_t[some, :], grads[:, aligned(start, blocks * 128)],
+                    preferred_element_type=F32,
+                )
+                for i in range(K2_ROWS // 128):
+                    for j in range(blocks):
+                        kept_in = keep_in[(half * 512 + r * K2_ROWS) // 128 + i, first + j]
+                        buf[
+                            r * K2_ROWS + i * 128 : r * K2_ROWS + i * 128 + 128,
+                            aligned(start + j * 128, 128),
+                        ] = v[i * 128 : i * 128 + 128, j * 128 : j * 128 + 128] * kept_in.astype(F32)
 
         @pl.loop(0, 3)
         def _(t):
@@ -587,10 +593,14 @@
 
     loads[0].wait()
     loads[1].wait()
+    for load in loads[2:4]:
+        load.start()
     part(0, gp, gate_grad)
     loads[2].wait()
+    loads[3].wait()
+    for load in loads[4:]:
+        load.start()
     part(0, up, up_grad)
-    loads[3].wait()
     loads[4].wait()
     loads[5].wait()
     passed = [

time: 225 us -> 220 us (0.978)
  Pallas kernels: 224 us -> 219 us
    pallas_call x1, Pallas kernels: 208 us -> 202 us  [forward(): pl.pallas_call(forward_kernel, out_shape=(sds((128, 1024), BF), sds((1024...]
where the time goes in v6:
time: 220 us
  Pallas kernels  219 us (100%)
    pallas_call x1, Pallas kernels, forward(): pl.pallas_call(forward_kernel, out_shape=(sds((128, 1024), BF), sds((1024...  202 us
    pallas_call x1, Pallas kernels, input_grads(): pl.pallas_call(input_grads_kernel, out_shape=(sds((1024, 896), F32), sds(...  16.4 us

profile of v6, /device:TPU:0, one launch (start us, length us, event | category | flops | bytes accessed | tf_op | source)
XLA Modules:
  0.0 219.6 jit_solution(16940338190010395602)
XLA Ops:
  0.6 202.4 %shard_map.102 = (bf16[128,1024]{1,0:T(8,128)(2,1)}, bf16[1024,2048]{1,0:T(8,128)(2,1)}, f32[896,1024]{1,0:T(8,128)}, bf16[2048,896]{1,0:T(8,128)(2,1)}, bf16[2048,896]{1,0:T(8,128)(2,1)}) custom-call(bf16[128,1024]{1,0:T(8,128)(2,1)} %tok.1, bf16[128,1024]{1,0:T(8,128)(2,1)} %cot.1, bf16[1024,896]{1,0:T(8,128)(2,1)} %gate_w.1, bf16[1024,896]{1,0:T(8,128)(2,1)} %up_w.1, ...), custom_call_target="tpu_custom_call" | custom-call | tf_op jit(solution)/shard_map/pallas_call | solution.py:522
  203.0 16.4 %shard_map.103 = (f32[1024,896]{1,0:T(8,128)}, f32[1024,896]{1,0:T(8,128)}, f32[896,1024]{1,0:T(8,128)}, bf16[128,1024]{1,0:T(8,128)(2,1)}) custom-call(s32[8,7]{1,0:T(8,128)} %keep_in.3, bf16[1024,2048]{1,0:T(8,128)(2,1)} %get-tuple-element.13.tok_t_hbm, bf16[2048,896]{1,0:T(8,128)(2,1)} %get-tuple-element.14.gp_hbm, ...), custom_call_target="tpu_custom_call" | custom-call | tf_op jit(solution)/shard_map/pallas_call | solution.py:621

commit v7 on v6

--- a/solution.py
+++ b/solution.py
@@ -475,8 +475,6 @@
     down_grad(3)
     down_grad(4)
     next(up)
-    down_grad(5)
-    down_grad(6)
     for copy in z_fin:
         copy.wait_recv()
 
@@ -491,6 +489,8 @@
     row_total(1 - yl, o_ys)
     o_over = send(o_ys, o_yr, yn)
     row_total(yl, o_own)
+    down_grad(5)
+    down_grad(6)
     o_over.wait_recv()
     out[...] = (o_own[...] + o_yr[...].astype(F32)).astype(BF)
     next(up)

time: 220 us -> 220 us (level)
  no operation moved by 1% of the time
where the time goes in v7:
time: 220 us
  Pallas kernels  219 us (100%)
    pallas_call x1, Pallas kernels, forward(): pl.pallas_call(forward_kernel, out_shape=(sds((128, 1024), BF), sds((1024...  202 us
    pallas_call x1, Pallas kernels, input_grads(): pl.pallas_call(input_grads_kernel, out_shape=(sds((1024, 896), F32), sds(...  16.4 us

profile of v7, /device:TPU:0, one launch (start us, length us, event | category | flops | bytes accessed | tf_op | source)
XLA Modules:
  0.0 219.6 jit_solution(15321913441770457792)
XLA Ops:
  0.6 202.4 %shard_map.102 = (bf16[128,1024]{1,0:T(8,128)(2,1)}, bf16[1024,2048]{1,0:T(8,128)(2,1)}, f32[896,1024]{1,0:T(8,128)}, bf16[2048,896]{1,0:T(8,128)(2,1)}, bf16[2048,896]{1,0:T(8,128)(2,1)}) custom-call(bf16[128,1024]{1,0:T(8,128)(2,1)} %tok.1, bf16[128,1024]{1,0:T(8,128)(2,1)} %cot.1, bf16[1024,896]{1,0:T(8,128)(2,1)} %gate_w.1, bf16[1024,896]{1,0:T(8,128)(2,1)} %up_w.1, ...), custom_call_target="tpu_custom_call" | custom-call | tf_op jit(solution)/shard_map/pallas_call | solution.py:522
  203.0 16.4 %shard_map.103 = (f32[1024,896]{1,0:T(8,128)}, f32[1024,896]{1,0:T(8,128)}, f32[896,1024]{1,0:T(8,128)}, bf16[128,1024]{1,0:T(8,128)(2,1)}) custom-call(s32[8,7]{1,0:T(8,128)} %keep_in.3, bf16[1024,2048]{1,0:T(8,128)(2,1)} %get-tuple-element.13.tok_t_hbm, bf16[2048,896]{1,0:T(8,128)(2,1)} %get-tuple-element.14.gp_hbm, ...), custom_call_target="tpu_custom_call" | custom-call | tf_op jit(solution)/shard_map/pallas_call | solution.py:621
